TPU v7x, 128 devices: a whole 4x4x4 slice. The times are simulated.
128 devices in a mesh: seq: 8 (over z, y_hi), expert: 16 (over y_lo, x, core).
Axes of the slice: x: 4, y: 4 (y_hi: 2, y_lo: 2; y = y_hi * 2 + y_lo), z: 4, core: 2. Of those that a mesh axis runs over, the one named last changes fastest.
Arguments:
- tokens: bfloat16 [131072, 1280], P(('seq', 'expert')), may hold values from -6 to 6
- slot_embed: bfloat16 [256, 1280], replicated, may hold values from -2 to 2
- w_in: bfloat16 [64, 1280, 3072], P('expert', None, 'seq'), may hold values from -0.15625 to 0.15625
- w_out: bfloat16 [64, 3072, 1280], P('expert', 'seq'), may hold values from -0.109375 to 0.109375
- cotangent: bfloat16 [131072, 1280], P(('seq', 'expert')), may hold values from -6 to 6
Outputs:
- token_grad: bfloat16 [131072, 1280], P(('seq', 'expert'))
- embed_grad: float32 [256, 1280], P(('seq', 'expert'))
- w_in_grad: bfloat16 [64, 1280, 3072], P('expert', None, 'seq')
- w_out_grad: bfloat16 [64, 3072, 1280], P('expert', 'seq')
All inputs are finite; a program needn't handle non-finite values.
Results may differ from a plain program's by a relative error of at most 0.02.
Values may be sent and summed in bfloat16 or wider, within the bound.
A program may use at most 128 MiB of HBM per device.

v0:
```python
import jax
import jax.numpy as jnp
from jax import lax
from jax.sharding import PartitionSpec as P


def rows_product(left, right):
    return lax.dot_general(
        left, right, (((0,), (0,)), ((), ())), preferred_element_type=jnp.float32
    )


def cols_product(left, right):
    return lax.dot_general(
        left, right, (((1,), (1,)), ((), ())), preferred_element_type=jnp.float32
    )


def slot_sums(weights, data):
    pieces = lax.psum_scatter(
        rows_product(weights, data), "expert", scatter_dimension=0, tiled=True
    )
    return lax.psum(pieces, "seq")


def slot_spread(partial_value):
    summed = lax.psum(partial_value, "seq").astype(jnp.bfloat16)
    return lax.all_gather(summed, "expert", axis=0, tiled=True)


def on_device(tokens, slot_embed, w_in, w_out, cotangent):
    width = tokens.shape[1]
    local_experts = w_in.shape[0]
    logits = cols_product(tokens, slot_embed)
    column_top = lax.pmax(jnp.max(logits, axis=0), ("seq", "expert"))
    raw_weights = jnp.exp(logits - column_top)
    column_sum = lax.psum(jnp.sum(raw_weights, axis=0), ("seq", "expert"))
    dispatch_f = raw_weights / column_sum
    dispatch = dispatch_f.astype(jnp.bfloat16)
    slot_in = slot_sums(dispatch, tokens).astype(jnp.bfloat16)
    grouped = slot_in.reshape(local_experts, -1, width)
    pre = jnp.einsum("esd,edf->esf", grouped, w_in, preferred_element_type=jnp.float32)
    hidden = jax.nn.gelu(pre, approximate=True).astype(jnp.bfloat16)
    out_part = jnp.einsum("esf,efd->esd", hidden, w_out, preferred_element_type=jnp.float32)
    slot_out = slot_spread(out_part.reshape(-1, width))
    combine_f = jax.nn.softmax(logits, axis=1)
    combine = combine_f.astype(jnp.bfloat16)
    comb_grad = cols_product(cotangent, slot_out)
    logit_comb = combine_f * (comb_grad - jnp.sum(combine_f * comb_grad, axis=1, keepdims=True))
    slot_grad = slot_sums(combine, cotangent).astype(jnp.bfloat16).reshape(local_experts, -1, width)
    w_out_grad = jnp.einsum(
        "esf,esd->efd", hidden, slot_grad, preferred_element_type=jnp.float32
    ).astype(jnp.bfloat16)
    hid_grad = jnp.einsum("esd,efd->esf", slot_grad, w_out, preferred_element_type=jnp.float32)
    pre_grad = jax.vjp(lambda v: jax.nn.gelu(v, approximate=True), pre)[1](hid_grad)[0].astype(
        jnp.bfloat16
    )
    w_in_grad = jnp.einsum(
        "esd,esf->edf", grouped, pre_grad, preferred_element_type=jnp.float32
    ).astype(jnp.bfloat16)
    in_part = jnp.einsum("esf,edf->esd", pre_grad, w_in, preferred_element_type=jnp.float32)
    in_grad = slot_spread(in_part.reshape(-1, width))
    disp_grad = cols_product(tokens, in_grad)
    inner = lax.psum(jnp.sum(dispatch_f * disp_grad, axis=0), ("seq", "expert"))
    logit_grad = (dispatch_f * (disp_grad - inner) + logit_comb).astype(jnp.bfloat16)
    token_grad = (
        jnp.dot(dispatch, in_grad, preferred_element_type=jnp.float32)
        + jnp.dot(logit_grad, slot_embed, preferred_element_type=jnp.float32)
    ).astype(jnp.bfloat16)
    embed_grad = lax.psum_scatter(
        rows_product(logit_grad, tokens), ("seq", "expert"), scatter_dimension=0, tiled=True
    )
    return (token_grad, embed_grad, w_in_grad, w_out_grad)


def solution(mesh):
    in_specs = (
        P(("seq", "expert"), None),
        P(),
        P("expert", None, "seq"),
        P("expert", "seq", None),
        P(("seq", "expert"), None),
    )
    out_specs = (
        P(("seq", "expert"), None),
        P(("seq", "expert"), None),
        P("expert", None, "seq"),
        P("expert", "seq", None),
    )
    return jax.shard_map(
        on_device, mesh=mesh, in_specs=in_specs, out_specs=out_specs, check_vma=False
    )
```

profile of v0, /device:TPU:1, one launch (start us, length us, event | category | flops | bytes accessed | tf_op | source)
XLA Modules:
  0.0 631.7 jit_solution(2113616563427907794)
XLA Ops:
  7.2 0.0 copy-start
  7.2 0.0 reduce-scatter.5.cloned.1.call-start
  7.2 1.7 copy-done
  8.9 3.0 fusion.24
  11.9 68.6 %pmax.7 = f32[256]{0:T(256)S(1)} all-reduce(f32[256]{0:T(256)S(1)} %get-tuple-element.9), channel_id=1, replica_groups=mesh['seq'=8,'expert'=16] {'seq','expert'}, use_global_device_ids=true, to_apply=%region_1.0 | all-reduce | flops 256 | bytes 2048 | tf_op jit(solution)/shard_map/pmax | solution.py:35
  80.5 1.6 fusion.3
  82.2 62.6 %psum.42 = f32[256]{0:T(256)S(1)} all-reduce(f32[256]{0:T(256)S(1)} %get-tuple-element.7), channel_id=1, replica_groups=mesh['seq'=8,'expert'=16] {'seq','expert'}, use_global_device_ids=true, to_apply=%region_3.0 | all-reduce | flops 256 | bytes 2048 | tf_op jit(solution)/shard_map/psum | solution.py:37
  144.8 3.2 fusion.8
  148.0 0.0 reduce-scatter.5.cloned.1.call-update
  148.0 0.0 reduce-scatter.3.cloned.1.call-start
  148.0 4.2 fusion.4
  152.3 0.0 reduce-scatter.3.cloned.1.call-update
  152.3 0.0 all-reduce.7.cloned.1.call-start
  152.3 51.3 %reduce-scatter.5.cloned.1.call-done = f32[16,1280]{1,0:T(8,128)} async-done(((f32[256,1280]{1,0:T(8,128)}), f32[16,1280]{1,0:T(8,128)}) %reduce-scatter.5.cloned.1.call-update) | async-done | bytes 81936 | tf_op jit(solution)/shard_map/reduce_scatter | solution.py:20
  203.6 63.3 %reduce-scatter.3.cloned.1.call-done = f32[16,1280]{1,0:T(8,128)} async-done(((f32[256,1280]{1,0:T(8,128)}), f32[16,1280]{1,0:T(8,128)}) %reduce-scatter.3.cloned.1.call-update) | async-done | bytes 81936 | tf_op jit(solution)/shard_map/reduce_scatter | solution.py:20
  266.9 38.6 %all-reduce.8 = (bf16[16,1280]{1,0:T(8,128)(2,1)S(1)}, bf16[16,1280]{1,0:T(8,128)(2,1)S(1)}) all-reduce(f32[16,1280]{1,0:T(8,128)} %reduce-scatter.5.cloned.1.call-done, f32[16,1280]{1,0:T(8,128)} %reduce-scatter.3.cloned.1.call-done), channel_id=1, replica_groups=mesh['seq'=8,'expert'=16] {'seq'}, use_global_device_ids=true, to_apply=%region_9.0 | all-reduce | flops 40960 | bytes 245760 | tf_op jit(solution)/shard_map/psum | solution.py:23
  305.6 0.0 copy-start.1
  305.6 2.9 fusion.26
  308.4 0.4 copy-done.1
  308.9 1.1 fusion.25
  310.0 0.0 copy-start.2
  310.0 0.6 fusion.17
  310.6 1.5 copy-done.2
  312.1 1.1 fusion.19
  313.2 3.2 convolution_convert_fusion.1
  316.5 32.1 %all-reduce.9 = (bf16[16,1280]{1,0:T(8,128)(2,1)S(1)}, bf16[16,1280]{1,0:T(8,128)(2,1)S(1)}) all-reduce(f32[16,1280]{1,0:T(8,128)S(1)} %reshape.28, f32[16,1280]{1,0:T(8,128)S(1)} %reshape.29), channel_id=1, replica_groups=mesh['seq'=8,'expert'=16] {'seq'}, use_global_device_ids=true, to_apply=%region_10.0 | all-reduce | flops 40960 | bytes 245760 | tf_op jit(solution)/shard_map/psum | solution.py:27
  348.7 35.7 %all_gather.6 = bf16[256,1280]{1,0:T(8,128)(2,1)S(1)} all-gather(bf16[16,1280]{1,0:T(8,128)(2,1)S(1)} %get-tuple-element.10), channel_id=1, replica_groups=mesh['seq'=8,'expert'=16] {'expert'}, dimensions={0}, use_global_device_ids=true | all-gather | bytes 696320 | tf_op jit(solution)/shard_map/all_gather | solution.py:28
  384.3 0.0 copy-start.3
  384.3 19.7 %all_gather.7 = bf16[256,1280]{1,0:T(8,128)(2,1)S(1)} all-gather(bf16[16,1280]{1,0:T(8,128)(2,1)S(1)} %get-tuple-element.11), channel_id=1, replica_groups=mesh['seq'=8,'expert'=16] {'expert'}, dimensions={0}, use_global_device_ids=true | all-gather | bytes 696320 | tf_op jit(solution)/shard_map/all_gather | solution.py:28
  404.0 2.6 convolution_bitcast_fusion
  406.6 0.0 copy-done.3
  406.6 0.0 copy-start.4
  406.6 3.2 fusion.6
  409.8 0.0 copy-done.4
  409.8 2.0 multiply_reduce_fusion.1
  411.8 62.5 %psum.46 = f32[256]{0:T(256)S(1)} all-reduce(f32[256]{0:T(256)S(1)} %get-tuple-element.4), channel_id=1, replica_groups=mesh['seq'=8,'expert'=16] {'seq','expert'}, use_global_device_ids=true, to_apply=%region_12.0 | all-reduce | flops 256 | bytes 2048 | tf_op jit(solution)/shard_map/psum | solution.py:64
  474.3 2.4 add_convert_fusion.1
  476.7 1.9 fusion.27
  478.6 0.0 all-reduce.7.cloned.1.call-update
  478.6 0.0 copy-start.5
  478.6 3.2 convolution_convert_fusion
  481.8 0.0 copy-done.5
  481.8 4.8 add_convert_fusion
  486.6 137.2 %all-reduce.7.cloned.1.call-done = f32[256,1280]{1,0:T(8,128)} async-done(((f32[256,1280]{1,0:T(8,128)}), f32[256,1280]{1,0:T(8,128)}) %all-reduce.7.cloned.1.call-update) | async-done | bytes 1310736
  623.8 1.4 constant_dynamic-slice_fusion
  (4 shorter events, 0.1 us)
Async XLA Ops:
  7.2 1.7 copy-start
  7.2 196.4 %reduce-scatter.5.cloned.1.call-start = ((), (), s32[]{:S(2)}) async-start(), calls=%async_computation.3 | async-start | bytes 1392640 | tf_op jit(solution)/shard_map/reduce_scatter | solution.py:20
  148.0 118.9 %reduce-scatter.3.cloned.1.call-start = ((), (), s32[]{:S(2)}) async-start(), calls=%async_computation.2 | async-start | bytes 1392640 | tf_op jit(solution)/shard_map/reduce_scatter | solution.py:20
  152.3 471.5 %all-reduce.7.cloned.1.call-start = ((), (), s32[]{:S(2)}) async-start(), calls=%async_computation.4 | async-start | bytes 2621440
  305.6 3.3 copy-start.1
  310.0 2.1 copy-start.2
  384.3 22.3 %copy-start.3 = (f32[1024,256]{1,0:T(8,128)S(1)}, f32[1024,256]{1,0:T(8,128)}, u32[]{:S(2)}) copy-start(f32[1024,256]{1,0:T(8,128)} %get-tuple-element.14) | copy-start | bytes 3145732
  406.6 3.2 copy-start.4
  478.6 3.2 copy-start.5
Sparse Core Ops, SparseCore 0:
  148.1 55.4 reduce-scatter.4
  206.6 60.2 reduce-scatter.2
  478.7 145.0 all-reduce.6
where the time goes:
time: 632 us
  blocking collectives  320 us (51%)
  waiting for transfers between devices  252 us (40%)
  matrix products  37.1 us (6%)
  between operations  13.9 us (2%)
    unnamed x4, waiting for transfers between devices  137 us
    reduce_scatter x2, waiting for transfers between devices, slot_sums(): lax.psum_scatter(rows_product(weights, data), 'expert', scatter_dimension...  115 us
    pmax x1, blocking collectives, on_device(): column_top = lax.pmax(jnp.max(logits, axis=0), ('seq', 'expert'))  68.6 us
    psum x1, blocking collectives, on_device(): column_sum = lax.psum(jnp.sum(raw_weights, axis=0), ('seq', 'expert'))  62.6 us
    psum x1, blocking collectives, on_device(): inner = lax.psum(jnp.sum(dispatch_f * disp_grad, axis=0), ('seq', 'expert'))  62.5 us
    all_gather x2, blocking collectives, slot_spread(): return lax.all_gather(summed, 'expert', axis=0, tiled=True)  55.3 us
    psum x1, blocking collectives, slot_sums(): return lax.psum(pieces, 'seq')  38.6 us
    psum x1, blocking collectives, slot_spread(): summed = lax.psum(partial_value, 'seq').astype(jnp.bfloat16)  32.1 us
  transfers between devices with their start and end apart: 3, of which 3 were waited for; matrix products, arithmetic and copies ran while one was open for 2% of the time, Pallas kernels for 0%

commit v1 on v0

v1 whole, which is shorter than its diff:
```python
import functools

import jax
import jax.numpy as jnp
from jax import lax
from jax.experimental import pallas as pl
from jax.experimental.pallas import tpu as pltpu
from jax.sharding import PartitionSpec as P

MESH = pl.DeviceIdType.MESH
F32 = jnp.float32
BF16 = jnp.bfloat16
CHUNK = 256
GELU_C = 0.7978845608028654
GELU_A = 0.044715


def coords():
    s = lax.axis_index("seq")
    e = lax.axis_index("expert")
    return s // 2, (s % 2) * 2 + e // 8, (e // 2) % 4, e % 2


def device(z, y, x, c):
    return (z * 2 + y // 2, (y % 2) * 8 + x * 2 + c)


def nn(a, b):
    return lax.dot_general(a, b, (((1,), (0,)), ((), ())), preferred_element_type=F32)


def nt(a, b):
    return lax.dot_general(a, b, (((1,), (1,)), ((), ())), preferred_element_type=F32)


def rows_at(start, size, unit):
    return pl.ds(pl.multiple_of(start, unit), size)


def split3(v):
    hi = v.astype(BF16).astype(F32)
    mid = (v - hi).astype(BF16).astype(F32)
    lo = (v - hi - mid).astype(BF16).astype(F32)
    return hi, mid, lo


def scalar_tile(columns):
    parts = [p for v in columns for p in split3(v)]
    rows = columns[0].shape[0]
    lane = lax.broadcasted_iota(jnp.int32, (rows, 128), 1)
    tile = jnp.zeros((rows, 128), F32)
    for i, p in enumerate(parts):
        tile = jnp.where((lane >= 16 * i) & (lane < 16 * i + 16), p, tile)
    return tile


def scalar_of(tile, i):
    a = 48 * i
    return tile[:, a : a + 1] + tile[:, a + 16 : a + 17] + tile[:, a + 32 : a + 33]


def chunk_tiles(v16, z):
    h, q = z // 2, z % 2
    return [v16[8 * h : 8 * h + 8, 640 * q + 128 * j : 640 * q + 128 * j + 128] for j in range(5)]


def unpack_rows(blocks):
    out = []
    for j in range(10):
        q, jj = j // 5, j % 5
        out.append(
            jnp.concatenate([blocks[q][8 * jj : 8 * jj + 8], blocks[2 + q][8 * jj : 8 * jj + 8]], axis=0)
        )
    return out


class Net:
    def __init__(self, ss, rs):
        self.ss, self.rs, self.count, self.all = ss, rs, 0, []

    def put(self, src, dst, dev):
        i = self.count
        self.count += 1
        copy = pltpu.make_async_remote_copy(
            src_ref=src, dst_ref=dst, send_sem=self.ss.at[i], recv_sem=self.rs.at[i],
            device_id=dev, device_id_type=MESH,
        )
        copy.start()
        self.all.append(copy)
        return copy


N_COPIES = 128
TILE0 = (8, 128)


def main_kernel(
    tok_h, emb_h, win_h, wout_h, cot_h,
    eg_o, lhs_o, rhs_o, sin_o, sgr_o, hid_o, pgr_o,
    tok, emb, win, wout, cot,
    lt, et, cf, cb, m_s, s_s,
    u_own, u_cs, u_cr, u_xs, u_xr, u_pk, u_yr, sall,
    g_own, g_cs, g_cr, g_pk, g_zr, g_pk2, g_yr, gall,
    o_pk, o_sr, oall, i_pk, i_sr, iall,
    l_all, inner_all,
    c_own, c_cs, c_cr, c_ys, c_yr, c_xs, c_xr, c_fs, c_fr,
    ld, ss, rs,
):
    z, y, x, c = coords()
    ylo, yhi = y % 2, y // 2
    oc = 1 - c
    D = tok.shape[1]
    net = Net(ss, rs)

    loads = {}

    def load(name, src, dst):
        cp = pltpu.make_async_copy(src, dst, ld.at[len(loads)])
        cp.start()
        loads[name] = cp

    for cc in range(2):
        for xx in range(4):
            for yy in range(2):
                g = yy * 8 + xx * 2 + cc
                p = cc * 128 + xx * 32 + yy * 16
                load(("emb", g), emb_h.at[pl.ds(16 * g, 16)], emb.at[pl.ds(p, 16)])
    n_chunks = tok.shape[0] // CHUNK
    for t in range(n_chunks):
        load(("tok", t), tok_h.at[pl.ds(t * CHUNK, CHUNK)], tok.at[pl.ds(t * CHUNK, CHUNK)])
    load("cot", cot_h, cot)
    load("win", win_h, win)
    load("wout", wout_h, wout)

    barrier = pltpu.get_barrier_semaphore()
    partners = [(z, y, x, oc)]
    partners += [((z + a) % 4, (y + b) % 4, x, c) for a in range(4) for b in range(4) if a or b]
    partners += [(z, (y + b) % 4, (x + a) % 4, c) for a in range(1, 4) for b in range(4)]
    for p in partners:
        pl.semaphore_signal(barrier, inc=1, device_id=device(*p), device_id_type=MESH)

    for g in range(16):
        loads[("emb", g)].wait()
    for t in range(n_chunks):
        loads[("tok", t)].wait()
        lt[:, t * CHUNK : (t + 1) * CHUNK] = nt(emb[...], tok[t * CHUNK : (t + 1) * CHUNK, :])

    @pl.loop(0, 8)
    def _(i):
        r = rows_at(i * 32, 32, 32)
        l = lt[r, :]
        m = jnp.max(l, axis=1, keepdims=True)
        e = jnp.exp(l - m)
        s = jnp.sum(e, axis=1, keepdims=True)
        et[r, :] = e.astype(BF16)
        m_s[r, :] = jnp.broadcast_to(m, (32, 128))
        s_s[r, :] = jnp.broadcast_to(s, (32, 128))

    ro = rows_at(oc * 128, 128, 128)
    rc = rows_at(c * 128, 128, 128)
    w_o = et[ro, :]
    for n in range(D // 256):
        u_cs[:, n * 256 : (n + 1) * 256] = nn(w_o, tok[:, n * 256 : (n + 1) * 256]).astype(BF16)
    u_cs[:, D : D + 128] = scalar_tile([m_s[ro, 0:1], s_s[ro, 0:1]]).astype(BF16)
    pl.semaphore_wait(barrier, len(partners))
    u_core = net.put(u_cs, u_cr, device(z, y, x, oc))
    w_c = et[rc, :]
    for n in range(D // 256):
        u_own[:, n * 256 : (n + 1) * 256] = nn(w_c, tok[:, n * 256 : (n + 1) * 256])

    @pl.loop(0, n_chunks)
    def _(t):
        k = rows_at(t * CHUNK, CHUNK, CHUNK)
        l = lt[:, k]
        e = jnp.exp(l - jnp.max(l, axis=0, keepdims=True))
        f = e / jnp.sum(e, axis=0, keepdims=True)
        cf[:, k] = f
        cb[:, k] = f.astype(BF16)

    u_core.wait_recv()

    @pl.loop(0, 8)
    def _(i):
        r = rows_at(i * 16, 16, 16)
        rg = rows_at(c * 128 + i * 16, 16, 16)
        v = u_cr[r, :].astype(F32)
        m1, s1 = m_s[rg, 0:1], s_s[rg, 0:1]
        sc = v[:, D : D + 128]
        m2, s2 = scalar_of(sc, 0), scalar_of(sc, 1)
        m = jnp.maximum(m1, m2)
        f1, f2 = jnp.exp(m1 - m), jnp.exp(m2 - m)
        s = s1 * f1 + s2 * f2
        u = u_own[r, :] * f1 + v[:, :D] * f2
        u_own[r, :] = u
        u_xs[r, :] = jnp.concatenate([u, scalar_tile([m, s])], axis=1).astype(BF16)
        m_s[rg, :] = jnp.broadcast_to(m, (16, 128))
        s_s[rg, :] = jnp.broadcast_to(s, (16, 128))

    u_x = []
    for k in range(1, 4):
        xx = (x + k) % 4
        u_x.append(net.put(u_xs.at[rows_at(xx * 32, 32, 32)], u_xr.at[k - 1], device(z, y, xx, c)))

    cot_load = loads["cot"]
    cot_load.wait()
    w_o = cb[ro, :]
    for n in range(D // 256):
        g_cs[:, n * 256 : (n + 1) * 256] = nn(w_o, cot[:, n * 256 : (n + 1) * 256]).astype(BF16)
    g_core = net.put(g_cs, g_cr, device(z, y, x, oc))
    w_c = cb[rc, :]
    for n in range(D // 256):
        g_own[:, n * 256 : (n + 1) * 256] = nn(w_c, cot[:, n * 256 : (n + 1) * 256])
    g_core.wait_recv()

    @pl.loop(0, 4)
    def _(i):
        r = rows_at(i * 32, 32, 32)
        v = g_own[r, :] + g_cr[r, :].astype(F32)
        for zz in range(4):
            tiles = chunk_tiles(v[:16], zz) + chunk_tiles(v[16:], zz)
            g_pk[zz, rows_at(i * 80, 80, 16), :] = jnp.concatenate(tiles, axis=0).astype(BF16)

    g_z = []
    for k in range(1, 4):
        zz = (z + k) % 4
        g_z.append(net.put(g_pk.at[zz], g_zr.at[k - 1], device(zz, y, x, c)))

    for cp in u_x:
        cp.wait_recv()
    for yy in range(2):
        r0 = x * 32 + yy * 16
        r = rows_at(r0, 16, 16)
        rg = rows_at(c * 128 + r0, 16, 16)
        ms, sums, us = [m_s[rg, 0:1]], [s_s[rg, 0:1]], [u_own[r, :]]
        for k in range(3):
            v = u_xr[k, yy * 16 : yy * 16 + 16, :].astype(F32)
            sc = v[:, D : D + 128]
            ms.append(scalar_of(sc, 0))
            sums.append(scalar_of(sc, 1))
            us.append(v[:, :D])
        m = functools.reduce(jnp.maximum, ms)
        fs = [jnp.exp(mk - m) for mk in ms]
        s = sum(a * f for a, f in zip(sums, fs))
        u = sum(a * f for a, f in zip(us, fs))
        for zz in range(4):
            h = zz // 2
            tile = scalar_tile([m[8 * h : 8 * h + 8], s[8 * h : 8 * h + 8]])
            u_pk[yy * 4 + zz] = jnp.concatenate(chunk_tiles(u, zz) + [tile], axis=0).astype(BF16)
    u_yz = []
    for a in range(4):
        for b in range(4):
            if a or b:
                zz, yy = (z + a) % 4, (y + b) % 4
                u_yz.append(net.put(u_pk.at[(yy % 2) * 4 + zz], u_yr.at[a * 4 + b], device(zz, yy, x, c)))
    u_yr[0] = u_pk[ylo * 4 + z]

    for cp in g_z:
        cp.wait_recv()

    @pl.loop(0, 4)
    def _(i):
        r = rows_at(i * 80, 80, 16)
        v = g_pk[z, r, :].astype(F32)
        for k in range(3):
            v = v + g_zr[k, r, :].astype(F32)
        pad = jnp.zeros(TILE0, F32)
        g_pk2[2 * i] = jnp.concatenate([v[:40], pad], axis=0).astype(BF16)
        g_pk2[2 * i + 1] = jnp.concatenate([v[40:], pad], axis=0).astype(BF16)

    g_xy = []
    for a in range(4):
        for b in range(4):
            if a or b:
                xx, yy = (x + a) % 4, (y + b) % 4
                g_xy.append(net.put(g_pk2.at[xx * 2 + yy % 2], g_yr.at[a * 4 + b], device(z, yy, xx, c)))
    g_yr[0] = g_pk2[x * 2 + ylo]

    for cp in u_yz:
        cp.wait_recv()
    parts = [u_yr[k].astype(F32) for k in range(16)]
    ms = [scalar_of(v[40:48], 0) for v in parts]
    sums = [scalar_of(v[40:48], 1) for v in parts]
    m = functools.reduce(jnp.maximum, ms)
    fs = [jnp.exp(mk - m) for mk in ms]
    s = sum(a * f for a, f in zip(sums, fs))
    lse = m + jnp.log(s)
    lse_tile = scalar_tile([lse])
    tiles = []
    for j in range(5):
        tiles.append(sum(v[8 * j : 8 * j + 8] * f for v, f in zip(parts, fs)) / s)
    sall[z] = jnp.concatenate(tiles + [lse_tile], axis=0).astype(BF16)
    u_ag = []
    for k in range(1, 4):
        u_ag.append(net.put(sall.at[z], sall.at[z], device((z + k) % 4, y, x, c)))
    loads["win"].wait()
    loads["wout"].wait()
    for cp in u_ag:
        cp.wait_recv()

    F = win.shape[2]
    expert_of = lax.broadcasted_iota(jnp.int32, (16, 1), 0) // 4
    slot_in = jnp.concatenate(unpack_rows([sall[k].astype(F32) for k in range(4)]), axis=1).astype(BF16)
    sin_o[...] = slot_in
    pre = jnp.zeros((16, F), F32)
    for e in range(4):
        pre = jnp.where(expert_of == e, nn(slot_in, win[e]), pre)
    th = jnp.tanh(GELU_C * (pre + GELU_A * pre * pre * pre))
    hidden_f = 0.5 * pre * (1.0 + th)
    slope = 0.5 * (1.0 + th) + 0.5 * pre * (1.0 - th * th) * GELU_C * (1.0 + 3.0 * GELU_A * pre * pre)
    hid_o[...] = hidden_f.astype(BF16)
    out_part = jnp.zeros((16, D), F32)
    for e in range(4):
        out_part += nn(jnp.where(expert_of == e, hidden_f, 0.0).astype(BF16), wout[e])
    pad = jnp.zeros(TILE0, F32)
    for zz in range(4):
        o_pk[zz] = jnp.concatenate(chunk_tiles(out_part, zz) + [pad], axis=0).astype(BF16)

    def seq_sums(pk, sr):
        cps = []
        for a in range(4):
            for b in range(2):
                if a or b:
                    zz = (z + a) % 4
                    cps.append(net.put(pk.at[zz], sr.at[a * 2 + b], device(zz, (y + 2 * b) % 4, x, c)))
        sr[0] = pk[z]
        return cps

    o_seq = seq_sums(o_pk, o_sr)

    for cp in g_xy:
        cp.wait_recv()
    acc = g_yr[0].astype(F32)
    for k in range(1, 16):
        acc = acc + g_yr[k].astype(F32)
    gall[z] = acc.astype(BF16)
    g_ag = []
    for k in range(1, 4):
        g_ag.append(net.put(gall.at[z], gall.at[z], device((z + k) % 4, y, x, c)))
    for cp in g_ag:
        cp.wait_recv()

    slot_grad = jnp.concatenate(unpack_rows([gall[k].astype(F32) for k in range(4)]), axis=1).astype(BF16)
    sgr_o[...] = slot_grad
    hid_grad = jnp.zeros((16, F), F32)
    for e in range(4):
        hid_grad = jnp.where(expert_of == e, nt(slot_grad, wout[e]), hid_grad)
    pre_grad = (hid_grad * slope).astype(BF16)
    pgr_o[...] = pre_grad
    in_part = jnp.zeros((16, D), F32)
    for e in range(4):
        in_part = jnp.where(expert_of == e, nt(pre_grad, win[e]), in_part)
    inner_part = jnp.sum(pre * pre_grad.astype(F32), axis=1, keepdims=True)
    for zz in range(4):
        h = zz // 2
        tile = scalar_tile([inner_part[8 * h : 8 * h + 8]])
        i_pk[zz] = jnp.concatenate(chunk_tiles(in_part, zz) + [tile], axis=0).astype(BF16)
    i_seq = seq_sums(i_pk, i_sr)

    for cp in o_seq:
        cp.wait_recv()
    acc = o_sr[0, 0:40, :].astype(F32)
    for k in range(1, 8):
        acc = acc + o_sr[k, 0:40, :].astype(F32)
    mine = c * 8 + x * 2 + ylo
    oall[mine, z] = jnp.concatenate([acc, lse_tile], axis=0).astype(BF16)
    o_1 = []
    for a in range(4):
        for b in range(2):
            if a or b:
                yy = y if b == 0 else yhi * 2 + 1 - ylo
                o_1.append(net.put(oall.at[mine, z], oall.at[mine, z], device((z + a) % 4, yy, x, c)))

    for cp in i_seq:
        cp.wait_recv()
    blocks = [i_sr[k].astype(F32) for k in range(8)]
    acc = sum(v[:40] for v in blocks)
    inner = sum(scalar_of(v[40:48], 0) for v in blocks)
    cz = c * 4 + z
    iall[cz, x * 2 + ylo] = jnp.concatenate([acc, scalar_tile([inner])], axis=0).astype(BF16)
    i_1 = []
    for a in range(4):
        for b in range(2):
            if a or b:
                yy = y if b == 0 else yhi * 2 + 1 - ylo
                ref = iall.at[cz, x * 2 + ylo]
                i_1.append(net.put(ref, ref, device(z, yy, (x + a) % 4, c)))

    for cp in o_1:
        cp.wait_recv()
    other = device(z, y, x, oc)
    o_2, o_3 = [], []
    ref = oall.at[pl.ds(c * 8 + x * 2, 2)]
    for k in range(1, 4):
        o_2.append(net.put(ref, ref, device(z, y, (x + k) % 4, c)))
    o_3.append(net.put(ref, ref, other))
    for cp in i_1:
        cp.wait_recv()
    i_2, i_3 = [], []
    ref = iall.at[cz]
    for k in range(1, 4):
        i_2.append(net.put(ref, ref, device((z + k) % 4, y, x, c)))
    i_3.append(net.put(ref, ref, other))
    for k in range(1, 4):
        o_2[k - 1].wait_recv()
        ref = oall.at[pl.ds(c * 8 + ((x - k + 4) % 4) * 2, 2)]
        o_3.append(net.put(ref, ref, other))
    for k in range(1, 4):
        i_2[k - 1].wait_recv()
        ref = iall.at[c * 4 + (z - k + 4) % 4]
        i_3.append(net.put(ref, ref, other))
    for cp in o_3:
        cp.wait_recv()

    half = rhs_o.shape[0] // 2

    @pl.loop(0, 16)
    def _(i):
        blocks = [oall[i, k].astype(F32) for k in range(4)]
        r = rows_at(i * 16, 16, 16)
        for j, t in enumerate(unpack_rows(blocks)):
            rhs_o[r, j * 128 : (j + 1) * 128] = t.astype(BF16)
        lse16 = jnp.concatenate([scalar_of(blocks[0][40:48], 0), scalar_of(blocks[2][40:48], 0)], axis=0)
        l_all[r, :] = jnp.broadcast_to(lse16, (16, 128))

    @pl.loop(0, n_chunks)
    def _(t):
        k = rows_at(t * CHUNK, CHUNK, CHUNK)
        cg = nt(rhs_o[0:half, :], cot[k, :])
        f = cf[:, k]
        cf[:, k] = f * (cg - jnp.sum(f * cg, axis=0, keepdims=True))

    for cp in i_3:
        cp.wait_recv()

    @pl.loop(0, 16)
    def _(i):
        cc, kk = i // 8, i % 8
        blocks = [iall[cc * 4 + k, kk].astype(F32) for k in range(4)]
        r = rows_at(i * 16, 16, 16)
        for j, t in enumerate(unpack_rows(blocks)):
            rhs_o[r, j * 128 : (j + 1) * 128] = t.astype(BF16)
        in16 = jnp.concatenate([scalar_of(blocks[0][40:48], 0), scalar_of(blocks[2][40:48], 0)], axis=0)
        inner_all[r, :] = jnp.broadcast_to(in16, (16, 128))

    rhs_o[half:, :] = emb[...]

    @pl.loop(0, n_chunks)
    def _(t):
        k = rows_at(t * CHUNK, CHUNK, CHUNK)
        dg = nt(rhs_o[0:half, :], tok[k, :])
        df = jnp.exp(lt[:, k] - l_all[:, 0:1])
        lhs_o[0:half, k] = df.astype(BF16)
        lhs_o[half:, k] = (df * (dg - inner_all[:, 0:1]) + cf[:, k]).astype(BF16)

    H = D // 2
    for a, b in ((0, 256), (256, 256), (512, 128)):
        w = tok[:, rows_at(oc * H + a, b, 128)]
        c_cs[:, a : a + b] = nn(lhs_o[half:, :], w).astype(BF16)
    c_core = net.put(c_cs, c_cr, other)
    for a, b in ((0, 256), (256, 256), (512, 128)):
        w = tok[:, rows_at(c * H + a, b, 128)]
        c_own[:, a : a + b] = nn(lhs_o[half:, :], w)
    c_core.wait_recv()

    @pl.loop(0, 16)
    def _(i):
        r = rows_at(i * 16, 16, 16)
        c_ys[r, :] = (c_own[r, :] + c_cr[r, :].astype(F32)).astype(BF16)

    def block_of(zz, yy):
        return rows_at((yy % 2) * 128 + ((zz % 2) * 2 + yy // 2) * 32 + (zz // 2) * 16, 16, 16)

    c_y = []
    for a in range(4):
        for b in range(4):
            if a or b:
                zz, yy = (z + a) % 4, (y + b) % 4
                c_y.append(net.put(c_ys.at[block_of(zz, yy)], c_yr.at[a * 4 + b], device(zz, yy, x, c)))
    c_yr[0] = c_ys[block_of(z, y), :]
    for cp in c_y:
        cp.wait_recv()
    acc = c_yr[0].astype(F32)
    for k in range(1, 16):
        acc = acc + c_yr[k].astype(F32)
    c_xs[...] = acc
    c_x = []
    for k in range(1, 4):
        c_x.append(net.put(c_xs, c_xr.at[k - 1], device(z, y, (x + k) % 4, c)))
    for cp in c_x:
        cp.wait_recv()
    c_fs[...] = c_xs[...] + c_xr[0] + c_xr[1] + c_xr[2]
    c_f = net.put(c_fs, c_fr, other)

    def my_rows(ref):
        v = ref[rows_at((x // 2) * 8, 8, 8), :]
        k = (x % 2) * 2 + c
        out = v[0:2]
        for i in range(1, 4):
            out = jnp.where(k == i, v[2 * i : 2 * i + 2], out)
        return out

    eg_o[:, rows_at(c * H, H, 128)] = my_rows(c_fs)
    c_f.wait_recv()
    eg_o[:, rows_at(oc * H, H, 128)] = my_rows(c_fr)

    for cp in net.all:
        cp.wait_send()


def on_device(tokens, slot_embed, w_in, w_out, cotangent):
    T, D = tokens.shape
    S = slot_embed.shape[0]
    E, _, F = w_in.shape
    V = pltpu.VMEM
    shape = jax.ShapeDtypeStruct
    blk = (48, 128)
    scratch = [
        V((T, D), BF16), V((S, D), BF16), V(w_in.shape, BF16), V(w_out.shape, BF16), V((T, D), BF16),
        V((S, T), F32), V((S, T), BF16), V((S, T), F32), V((S, T), BF16), V((S, 128), F32), V((S, 128), F32),
        V((128, D), F32), V((128, D + 128), BF16), V((128, D + 128), BF16),
        V((128, D + 128), BF16), V((3, 32, D + 128), BF16), V((8,) + blk, BF16), V((16,) + blk, BF16), V((4,) + blk, BF16),
        V((128, D), F32), V((128, D), BF16), V((128, D), BF16), V((4, 320, 128), BF16), V((3, 320, 128), BF16),
        V((8,) + blk, BF16), V((16,) + blk, BF16), V((4,) + blk, BF16),
        V((4,) + blk, BF16), V((8,) + blk, BF16), V((16, 4) + blk, BF16),
        V((4,) + blk, BF16), V((8,) + blk, BF16), V((8, 8) + blk, BF16),
        V((S, 128), F32), V((S, 128), F32),
        V((S, D // 2), F32), V((S, D // 2), BF16), V((S, D // 2), BF16), V((S, D // 2), BF16),
        V((16, 16, D // 2), BF16), V((16, D // 2), F32), V((3, 16, D // 2), F32), V((16, D // 2), F32), V((16, D // 2), F32),
        pltpu.SemaphoreType.DMA((32,)),
        pltpu.SemaphoreType.DMA((N_COPIES,)),
        pltpu.SemaphoreType.DMA((N_COPIES,)),
    ]
    eg, lhs, rhs, slot_in, slot_grad, hidden, pre_grad = pl.pallas_call(
        main_kernel,
        name="moe_exchange",
        out_shape=[
            shape((2, D), F32), shape((2 * S, T), BF16), shape((2 * S, D), BF16),
            shape((16, D), BF16), shape((16, D), BF16), shape((16, F), BF16), shape((16, F), BF16),
        ],
        in_specs=[pl.BlockSpec(memory_space=pl.ANY)] * 5,
        out_specs=[pl.BlockSpec(memory_space=pltpu.VMEM)] * 7,
        scratch_shapes=scratch,
        compiler_params=pltpu.CompilerParams(
            collective_id=0, has_side_effects=True, vmem_limit_bytes=60 * 2**20
        ),
    )(tokens, slot_embed, w_in, w_out, cotangent)
    token_grad = lax.dot_general(lhs, rhs, (((0,), (0,)), ((), ())), preferred_element_type=F32).astype(BF16)

    def grouped(v):
        return v.reshape(E, -1, v.shape[1])

    w_out_grad = jnp.einsum(
        "esf,esd->efd", grouped(hidden), grouped(slot_grad), preferred_element_type=F32
    ).astype(BF16)
    w_in_grad = jnp.einsum(
        "esd,esf->edf", grouped(slot_in), grouped(pre_grad), preferred_element_type=F32
    ).astype(BF16)
    return (token_grad, eg, w_in_grad, w_out_grad)


def solution(mesh):
    in_specs = (
        P(("seq", "expert"), None),
        P(),
        P("expert", None, "seq"),
        P("expert", "seq", None),
        P(("seq", "expert"), None),
    )
    out_specs = (
        P(("seq", "expert"), None),
        P(("seq", "expert"), None),
        P("expert", None, "seq"),
        P("expert", "seq", None),
    )
    return jax.shard_map(
        on_device, mesh=mesh, in_specs=in_specs, out_specs=out_specs, check_vma=False
    )
```

time: 632 us -> 98.9 us (0.16)
  blocking collectives: 320 us -> 0 us
  waiting for transfers between devices: 252 us -> 0 us
  Pallas kernels: 0 us -> 83.2 us
  matrix products: 37.1 us -> 11.1 us
  between operations: 13.9 us -> 0.64 us
    psum x4 -> x0, blocking collectives: 196 us -> none  [the longest x1 62.6 us: on_device(): column_sum = lax.psum(jnp.sum(raw_weights, axis=0), ('seq', 'expert'))]
    unnamed x4 -> x0, waiting for transfers between devices: 137 us -> none
    reduce_scatter x2 -> x0, waiting for transfers between devices: 115 us -> none  [slot_sums(): lax.psum_scatter(rows_product(weights, data), 'expert', scatter_dimension...]
    pallas_call x0 -> x1, Pallas kernels: none -> 83.2 us  [on_device(): pl.pallas_call(main_kernel, name='moe_exchange', out_shape=[shape((2, D),...]
    pmax x1 -> x0, blocking collectives: 68.6 us -> none  [on_device(): column_top = lax.pmax(jnp.max(logits, axis=0), ('seq', 'expert'))]
    all_gather x2 -> x0, blocking collectives: 55.3 us -> none  [slot_spread(): return lax.all_gather(summed, 'expert', axis=0, tiled=True)]
    dot_general x14 -> x3, matrix products: 37.1 us -> 11.1 us  [the longest x1 4.69 us: on_device(): lax.dot_general(lhs, rhs, (((0,), (0,)), ((), ())), preferred_element_typ...]
  transfers between devices with their start and end apart: 3 -> 0, of which waited for: 3 -> 0; matrix products, arithmetic and copies ran while one was open for 2% -> 0% of each run, Pallas kernels for 0% -> 0%
where the time goes in v1:
time: 98.9 us; the launch traced here: 98.5 us
  Pallas kernels  83.2 us (84%)
  matrix products  11.1 us (11%)
  local copies, waits for them, and re-layouts  3.62 us (4%)
    pallas_call x1, Pallas kernels, on_device(): pl.pallas_call(main_kernel, name='moe_exchange', out_shape=[shape((2, D),...  83.2 us
    dot_general x1, matrix products, on_device(): lax.dot_general(lhs, rhs, (((0,), (0,)), ((), ())), preferred_element_typ...  4.69 us
    dot_general x1, matrix products, on_device(): jnp.einsum('esd,esf->edf', grouped(slot_in), grouped(pre_grad), preferred...  3.21 us
    dot_general x1, matrix products, on_device(): jnp.einsum('esf,esd->efd', grouped(hidden), grouped(slot_grad), preferred...  3.16 us
    reshape x4, local copies, waits for them, and re-layouts, grouped(): return v.reshape(E, -1, v.shape[1])  3.02 us

profile of v1, /device:TPU:1, one launch (start us, length us, event | category | flops | bytes accessed | tf_op | source)
XLA Modules:
  0.0 98.5 jit_solution(5062793737961196326)
XLA Ops:
  0.6 83.2 %moe_exchange.1 = (f32[2,1280]{1,0:T(2,128)}, bf16[512,1024]{1,0:T(8,128)(2,1)}, bf16[512,1280]{1,0:T(8,128)(2,1)}, bf16[16,1280]{1,0:T(8,128)(2,1)}, bf16[16,12...) custom-call(bf16[1024,1280]{1,0:T(8,128)(2,1)} %tok_h.1, bf16[256,1280]{1,0:T(8,128)(2,1)} %emb_h.1, ...), custom_call_target="tpu_custom_call" | custom-call | tf_op jit(solution)/shard_map/moe_exchange/pallas_call | solution.py:533
  83.8 0.7 reshape.21
  84.5 0.7 reshape.22
  85.3 0.8 reshape.20
  86.1 0.8 reshape.23
  86.9 4.7 %convolution_convert_fusion.2 = bf16[1024,1280]{1,0:T(8,128)(2,1)} fusion(bf16[512,1024]{1,0:T(8,128)(2,1)} %get-tuple-element.11, bf16[512,1280]{1,0:T(8,128)(2,1)} %get-tuple-element.12), kind=kOutput, calls=%fused_computation.2 | convolution fusion | flops 1343488000 | bytes 4980736 | tf_op jit(solution)/shard_map/dot_general | solution.py:547
  91.5 0.0 copy-start
  91.6 3.2 %convolution_convert_fusion = bf16[4,384,1280]{2,1,0:T(8,128)(2,1)} fusion(bf16[4,4,384]{2,1,0:T(4,128)(2,1)S(1)} %reshape.22, bf16[4,4,1280]{2,1,0:T(4,128)(2,1)S(1)} %reshape.23), kind=kOutput, calls=%fused_computation | convolution fusion | flops 17694720 | bytes 3985408 | tf_op jit(solution)/shard_map/esf,esd->efd/dot_general | solution.py:552
  94.7 3.2 %convolution_convert_fusion.1 = bf16[4,1280,384]{2,1,0:T(8,128)(2,1)} fusion(bf16[4,4,1280]{2,1,0:T(4,128)(2,1)S(1)} %reshape.20, bf16[4,4,384]{2,1,0:T(4,128)(2,1)S(1)} %reshape.21), kind=kOutput, calls=%fused_computation.1 | convolution fusion | flops 17694720 | bytes 3985408 | tf_op jit(solution)/shard_map/esd,esf->edf/dot_general | solution.py:555
  97.9 0.0 copy-done
  97.9 0.6 copy.10
Async XLA Ops:
  91.5 6.4 %copy-start = (f32[2,1280]{1,0:T(2,128)S(1)}, f32[2,1280]{1,0:T(2,128)}, u32[]{:S(2)}) copy-start(f32[2,1280]{1,0:T(2,128)} %get-tuple-element.23) | copy-start | bytes 30724

commit v2 on v1

v2 whole, which is shorter than its diff:
```python
import functools

import jax
import jax.numpy as jnp
from jax import lax
from jax.experimental import pallas as pl
from jax.experimental.pallas import tpu as pltpu
from jax.sharding import PartitionSpec as P

MESH = pl.DeviceIdType.MESH
F32 = jnp.float32
BF16 = jnp.bfloat16
CHUNK = 256
GELU_C = 0.7978845608028654
GELU_A = 0.044715


def coords():
    s = lax.axis_index("seq")
    e = lax.axis_index("expert")
    return s // 2, (s % 2) * 2 + e // 8, (e // 2) % 4, e % 2


def device(z, y, x, c):
    return (z * 2 + y // 2, (y % 2) * 8 + x * 2 + c)


def nn(a, b):
    return lax.dot_general(a, b, (((1,), (0,)), ((), ())), preferred_element_type=F32)


def nt(a, b):
    return lax.dot_general(a, b, (((1,), (1,)), ((), ())), preferred_element_type=F32)


def rows_at(start, size, unit):
    return pl.ds(pl.multiple_of(start, unit), size)


def split3(v):
    hi = v.astype(BF16).astype(F32)
    mid = (v - hi).astype(BF16).astype(F32)
    lo = (v - hi - mid).astype(BF16).astype(F32)
    return hi, mid, lo


def scalar_tile(columns):
    parts = [p for v in columns for p in split3(v)]
    rows = columns[0].shape[0]
    lane = lax.broadcasted_iota(jnp.int32, (rows, 128), 1)
    tile = jnp.zeros((rows, 128), F32)
    for i, p in enumerate(parts):
        tile = jnp.where((lane >= 16 * i) & (lane < 16 * i + 16), p, tile)
    return tile


def scalar_of(tile, i):
    a = 48 * i
    return tile[:, a : a + 1] + tile[:, a + 16 : a + 17] + tile[:, a + 32 : a + 33]


def chunk_tiles(v16, z):
    h, q = z // 2, z % 2
    return [v16[8 * h : 8 * h + 8, 640 * q + 128 * j : 640 * q + 128 * j + 128] for j in range(5)]


def unpack_rows(blocks):
    out = []
    for j in range(10):
        q, jj = j // 5, j % 5
        out.append(
            jnp.concatenate([blocks[q][8 * jj : 8 * jj + 8], blocks[2 + q][8 * jj : 8 * jj + 8]], axis=0)
        )
    return out


class Group:
    def __init__(self, net, index, total):
        self.net, self.index, self.total = net, index, total

    def copy(self, src, dst, dev):
        return pltpu.make_async_remote_copy(
            src_ref=src, dst_ref=dst, send_sem=self.net.ss.at[self.index], recv_sem=self.net.rs.at[self.index],
            device_id=dev, device_id_type=MESH,
        )

    def put(self, src, dst, dev):
        self.copy(src, dst, dev).start()

    def wait_recv(self):
        self.copy(self.total, self.total, self.net.other).wait_recv()

    def wait_send(self):
        self.copy(self.total, self.total, self.net.other).wait_send()


class Net:
    def __init__(self, ss, rs, other):
        self.ss, self.rs, self.other, self.groups = ss, rs, other, []

    def group(self, total):
        g = Group(self, len(self.groups), total)
        self.groups.append(g)
        return g

    def put(self, src, dst, dev):
        g = self.group(dst)
        g.put(src, dst, dev)
        return g


N_GROUPS = 29
TILE0 = (8, 128)


def main_kernel(
    tok_h, emb_h, win_h, wout_h, cot_h,
    eg_o, lhs_o, rhs_o, sin_o, sgr_o, hid_o, pgr_o,
    tok, emb, win, wout, cot,
    lt, et, cf, cb, m_s, s_s,
    u_own, u_cs, u_cr, u_xs, u_xr, u_pk, u_yr, sall,
    g_own, g_cs, g_cr, g_pk, g_zr, g_pk2, g_yr, gall,
    o_pk, o_sr, oall, i_pk, i_sr, iall,
    l_all, inner_all,
    c_own, c_cs, c_cr, c_ys, c_yr, c_xs, c_xr,
    ld, ss, rs,
):
    z, y, x, c = coords()
    ylo, yhi = y % 2, y // 2
    oc = 1 - c
    D = tok.shape[1]
    other = device(z, y, x, oc)
    net = Net(ss, rs, other)

    loads = {}

    def load(name, src, dst):
        cp = pltpu.make_async_copy(src, dst, ld.at[len(loads)])
        cp.start()
        loads[name] = cp

    for cc in range(2):
        for xx in range(4):
            for yy in range(2):
                g = yy * 8 + xx * 2 + cc
                p = cc * 128 + xx * 32 + yy * 16
                pltpu.make_async_copy(emb_h.at[pl.ds(16 * g, 16)], emb.at[pl.ds(p, 16)], ld.at[0]).start()
    loads["emb"] = pltpu.make_async_copy(emb_h, emb, ld.at[0])
    n_chunks = tok.shape[0] // CHUNK
    for t in range(n_chunks):
        load(("tok", t), tok_h.at[pl.ds(t * CHUNK, CHUNK)], tok.at[pl.ds(t * CHUNK, CHUNK)])
    load("cot", cot_h, cot)
    load("win", win_h, win)
    load("wout", wout_h, wout)

    barrier = pltpu.get_barrier_semaphore()
    partners = [(z, y, x, oc)]
    partners += [((z + a) % 4, (y + b) % 4, x, c) for a in range(4) for b in range(4) if a or b]
    partners += [(z, (y + b) % 4, (x + a) % 4, c) for a in range(1, 4) for b in range(4)]
    partners += [(z, y, (x + a) % 4, oc) for a in range(1, 4)]
    for p in partners:
        pl.semaphore_signal(barrier, inc=1, device_id=device(*p), device_id_type=MESH)

    loads["emb"].wait()
    for t in range(n_chunks):
        loads[("tok", t)].wait()
        lt[:, t * CHUNK : (t + 1) * CHUNK] = nt(emb[...], tok[t * CHUNK : (t + 1) * CHUNK, :])

    @pl.loop(0, 8, unroll=4)
    def _(i):
        r = rows_at(i * 32, 32, 32)
        l = lt[r, :]
        m = jnp.max(l, axis=1, keepdims=True)
        e = jnp.exp(l - m)
        s = jnp.sum(e, axis=1, keepdims=True)
        et[r, :] = e.astype(BF16)
        m_s[r, :] = jnp.broadcast_to(m, (32, 128))
        s_s[r, :] = jnp.broadcast_to(s, (32, 128))

    ro = rows_at(oc * 128, 128, 128)
    rc = rows_at(c * 128, 128, 128)
    w_o = et[ro, :]
    for n in range(D // 256):
        u_cs[:, n * 256 : (n + 1) * 256] = nn(w_o, tok[:, n * 256 : (n + 1) * 256]).astype(BF16)
    u_cs[:, D : D + 128] = scalar_tile([m_s[ro, 0:1], s_s[ro, 0:1]]).astype(BF16)
    pl.semaphore_wait(barrier, len(partners))
    u_core = net.put(u_cs, u_cr, device(z, y, x, oc))
    w_c = et[rc, :]
    for n in range(D // 256):
        u_own[:, n * 256 : (n + 1) * 256] = nn(w_c, tok[:, n * 256 : (n + 1) * 256])

    @pl.loop(0, n_chunks)
    def _(t):
        k = rows_at(t * CHUNK, CHUNK, CHUNK)
        l = lt[:, k]
        e = jnp.exp(l - jnp.max(l, axis=0, keepdims=True))
        f = e / jnp.sum(e, axis=0, keepdims=True)
        cf[:, k] = f
        cb[:, k] = f.astype(BF16)

    u_core.wait_recv()

    @pl.loop(0, 8, unroll=4)
    def _(i):
        r = rows_at(i * 16, 16, 16)
        rg = rows_at(c * 128 + i * 16, 16, 16)
        v = u_cr[r, :].astype(F32)
        m1, s1 = m_s[rg, 0:1], s_s[rg, 0:1]
        sc = v[:, D : D + 128]
        m2, s2 = scalar_of(sc, 0), scalar_of(sc, 1)
        m = jnp.maximum(m1, m2)
        f1, f2 = jnp.exp(m1 - m), jnp.exp(m2 - m)
        s = s1 * f1 + s2 * f2
        u = u_own[r, :] * f1 + v[:, :D] * f2
        u_own[r, :] = u
        u_xs[r, :] = jnp.concatenate([u, scalar_tile([m, s])], axis=1).astype(BF16)
        m_s[rg, :] = jnp.broadcast_to(m, (16, 128))
        s_s[rg, :] = jnp.broadcast_to(s, (16, 128))

    u_x = net.group(u_xr)
    for k in range(1, 4):
        xx = (x + k) % 4
        u_x.put(u_xs.at[rows_at(xx * 32, 32, 32)], u_xr.at[k - 1], device(z, y, xx, c))

    cot_load = loads["cot"]
    cot_load.wait()
    w_o = cb[ro, :]
    for n in range(D // 256):
        g_cs[:, n * 256 : (n + 1) * 256] = nn(w_o, cot[:, n * 256 : (n + 1) * 256]).astype(BF16)
    g_core = net.put(g_cs, g_cr, device(z, y, x, oc))
    w_c = cb[rc, :]
    for n in range(D // 256):
        g_own[:, n * 256 : (n + 1) * 256] = nn(w_c, cot[:, n * 256 : (n + 1) * 256])
    g_core.wait_recv()

    @pl.loop(0, 4, unroll=2)
    def _(i):
        r = rows_at(i * 32, 32, 32)
        v = g_own[r, :] + g_cr[r, :].astype(F32)
        for zz in range(4):
            tiles = chunk_tiles(v[:16], zz) + chunk_tiles(v[16:], zz)
            g_pk[zz, rows_at(i * 80, 80, 16), :] = jnp.concatenate(tiles, axis=0).astype(BF16)

    g_z = net.group(g_zr)
    for k in range(1, 4):
        zz = (z + k) % 4
        g_z.put(g_pk.at[zz], g_zr.at[k - 1], device(zz, y, x, c))

    u_x.wait_recv()
    for yy in range(2):
        r0 = x * 32 + yy * 16
        r = rows_at(r0, 16, 16)
        rg = rows_at(c * 128 + r0, 16, 16)
        ms, sums, us = [m_s[rg, 0:1]], [s_s[rg, 0:1]], [u_own[r, :]]
        for k in range(3):
            v = u_xr[k, yy * 16 : yy * 16 + 16, :].astype(F32)
            sc = v[:, D : D + 128]
            ms.append(scalar_of(sc, 0))
            sums.append(scalar_of(sc, 1))
            us.append(v[:, :D])
        m = functools.reduce(jnp.maximum, ms)
        fs = [jnp.exp(mk - m) for mk in ms]
        s = sum(a * f for a, f in zip(sums, fs))
        u = sum(a * f for a, f in zip(us, fs))
        for zz in range(4):
            h = zz // 2
            tile = scalar_tile([m[8 * h : 8 * h + 8], s[8 * h : 8 * h + 8]])
            u_pk[yy * 4 + zz] = jnp.concatenate(chunk_tiles(u, zz) + [tile], axis=0).astype(BF16)
    u_yz = net.group(u_yr.at[pl.ds(1, 15)])
    for a in range(4):
        for b in range(4):
            if a or b:
                zz, yy = (z + a) % 4, (y + b) % 4
                u_yz.put(u_pk.at[(yy % 2) * 4 + zz], u_yr.at[a * 4 + b], device(zz, yy, x, c))
    u_yr[0] = u_pk[ylo * 4 + z]

    g_z.wait_recv()

    @pl.loop(0, 4, unroll=2)
    def _(i):
        r = rows_at(i * 80, 80, 16)
        v = g_pk[z, r, :].astype(F32)
        for k in range(3):
            v = v + g_zr[k, r, :].astype(F32)
        pad = jnp.zeros(TILE0, F32)
        g_pk2[2 * i] = jnp.concatenate([v[:40], pad], axis=0).astype(BF16)
        g_pk2[2 * i + 1] = jnp.concatenate([v[40:], pad], axis=0).astype(BF16)

    g_xy = net.group(g_yr.at[pl.ds(1, 15)])
    for a in range(4):
        for b in range(4):
            if a or b:
                xx, yy = (x + a) % 4, (y + b) % 4
                g_xy.put(g_pk2.at[xx * 2 + yy % 2], g_yr.at[a * 4 + b], device(z, yy, xx, c))
    g_yr[0] = g_pk2[x * 2 + ylo]

    u_yz.wait_recv()
    parts = [u_yr[k].astype(F32) for k in range(16)]
    ms = [scalar_of(v[40:48], 0) for v in parts]
    sums = [scalar_of(v[40:48], 1) for v in parts]
    m = functools.reduce(jnp.maximum, ms)
    fs = [jnp.exp(mk - m) for mk in ms]
    s = sum(a * f for a, f in zip(sums, fs))
    lse = m + jnp.log(s)
    lse_tile = scalar_tile([lse])
    tiles = []
    for j in range(5):
        tiles.append(sum(v[8 * j : 8 * j + 8] * f for v, f in zip(parts, fs)) / s)
    sall[z] = jnp.concatenate(tiles + [lse_tile], axis=0).astype(BF16)
    u_ag = net.group(sall.at[pl.ds(0, 3)])
    for k in range(1, 4):
        u_ag.put(sall.at[z], sall.at[z], device((z + k) % 4, y, x, c))

    g_xy.wait_recv()
    acc = g_yr[0].astype(F32)
    for k in range(1, 16):
        acc = acc + g_yr[k].astype(F32)
    gall[z] = acc.astype(BF16)
    g_ag = net.group(gall.at[pl.ds(0, 3)])
    for k in range(1, 4):
        g_ag.put(gall.at[z], gall.at[z], device((z + k) % 4, y, x, c))
    loads["win"].wait()
    loads["wout"].wait()
    u_ag.wait_recv()

    F = win.shape[2]
    expert_of = lax.broadcasted_iota(jnp.int32, (16, 1), 0) // 4
    slot_in = jnp.concatenate(unpack_rows([sall[k].astype(F32) for k in range(4)]), axis=1).astype(BF16)
    sin_o[...] = slot_in
    pre = jnp.zeros((16, F), F32)
    for e in range(4):
        pre = jnp.where(expert_of == e, nn(slot_in, win[e]), pre)
    th = jnp.tanh(GELU_C * (pre + GELU_A * pre * pre * pre))
    hidden_f = 0.5 * pre * (1.0 + th)
    slope = 0.5 * (1.0 + th) + 0.5 * pre * (1.0 - th * th) * GELU_C * (1.0 + 3.0 * GELU_A * pre * pre)
    hid_o[...] = hidden_f.astype(BF16)
    out_part = jnp.zeros((16, D), F32)
    for e in range(4):
        out_part += nn(jnp.where(expert_of == e, hidden_f, 0.0).astype(BF16), wout[e])
    for zz in range(4):
        tile = sall[zz, 40:48, :].astype(F32)
        o_pk[zz] = jnp.concatenate(chunk_tiles(out_part, zz) + [tile], axis=0).astype(BF16)

    def seq_sums(pk, sr):
        group = net.group(sr.at[pl.ds(1, 15)])
        for a in range(4):
            for b in range(4):
                if a or b:
                    zz = (z + a) % 4
                    group.put(pk.at[zz], sr.at[a * 4 + b], device(zz, (y + b) % 4, x, c))
        sr[0] = pk[z]
        return group

    def seq_total(sr, parity, rows):
        ks = [a * 4 + b for a in range(4) for b in range(4) if b % 2 == parity]
        acc = sr[ks[0], 0:rows, :].astype(F32)
        for k in ks[1:]:
            acc = acc + sr[k, 0:rows, :].astype(F32)
        return acc

    o_seq = seq_sums(o_pk, o_sr)

    g_ag.wait_recv()

    slot_grad = jnp.concatenate(unpack_rows([gall[k].astype(F32) for k in range(4)]), axis=1).astype(BF16)
    sgr_o[...] = slot_grad
    hid_grad = jnp.zeros((16, F), F32)
    for e in range(4):
        hid_grad = jnp.where(expert_of == e, nt(slot_grad, wout[e]), hid_grad)
    pre_grad = (hid_grad * slope).astype(BF16)
    pgr_o[...] = pre_grad
    in_part = jnp.zeros((16, D), F32)
    for e in range(4):
        in_part = jnp.where(expert_of == e, nt(pre_grad, win[e]), in_part)
    inner_part = jnp.sum(pre * pre_grad.astype(F32), axis=1, keepdims=True)
    for zz in range(4):
        h = zz // 2
        tile = scalar_tile([inner_part[8 * h : 8 * h + 8]])
        i_pk[zz] = jnp.concatenate(chunk_tiles(in_part, zz) + [tile], axis=0).astype(BF16)
    i_seq = seq_sums(i_pk, i_sr)

    o_seq.wait_recv()
    pair = c * 8 + x * 2
    for parity in range(2):
        acc = seq_total(o_sr, parity, 40)
        lse_tile = o_sr[parity, 40:48, :].astype(F32)
        oall[pair + (ylo + parity) % 2, z] = jnp.concatenate([acc, lse_tile], axis=0).astype(BF16)
    o_1 = net.group(oall.at[pl.ds(0, 2), pl.ds(0, 3)])
    for k in range(1, 4):
        ref = oall.at[pl.ds(pair, 2), z]
        o_1.put(ref, ref, device((z + k) % 4, y, x, c))

    i_seq.wait_recv()
    cz = c * 4 + z
    for parity in range(2):
        acc = seq_total(i_sr, parity, 48)
        inner = scalar_of(acc[40:48], 0)
        block = jnp.concatenate([acc[:40], scalar_tile([inner])], axis=0)
        iall[cz, x * 2 + (ylo + parity) % 2] = block.astype(BF16)
    i_1 = net.group(iall.at[0, pl.ds(0, 6)])
    for k in range(1, 4):
        ref = iall.at[cz, pl.ds(x * 2, 2)]
        i_1.put(ref, ref, device(z, y, (x + k) % 4, c))

    half = rhs_o.shape[0] // 2

    def place(i, blocks, scalars):
        r = rows_at(i * 16, 16, 16)
        for j, t in enumerate(unpack_rows(blocks)):
            rhs_o[r, j * 128 : (j + 1) * 128] = t.astype(BF16)
        v = jnp.concatenate([scalar_of(blocks[0][40:48], 0), scalar_of(blocks[2][40:48], 0)], axis=0)
        scalars[r, :] = jnp.broadcast_to(v, (16, 128))

    def place_out(first):
        for i in range(2):
            place(first + i, [oall[first + i, k].astype(F32) for k in range(4)], l_all)

    def place_in(core):
        @pl.loop(0, 8, unroll=4)
        def _(k):
            place(core * 8 + k, [iall[core * 4 + zz, k].astype(F32) for zz in range(4)], inner_all)

    o_1.wait_recv()
    o_2, o_3 = [], []
    ref = oall.at[pl.ds(pair, 2)]
    for k in range(1, 4):
        o_2.append(net.put(ref, ref, device(z, y, (x + k) % 4, c)))
    o_3.append(net.put(ref, ref, other))
    place_out(pair)
    i_1.wait_recv()
    i_2, i_3 = [], []
    ref = iall.at[cz]
    for k in range(1, 4):
        i_2.append(net.put(ref, ref, device((z + k) % 4, y, x, c)))
    i_3.append(net.put(ref, ref, other))
    for k in range(1, 4):
        o_2[k - 1].wait_recv()
        first = c * 8 + ((x - k + 4) % 4) * 2
        ref = oall.at[pl.ds(first, 2)]
        o_3.append(net.put(ref, ref, other))
        place_out(first)
    for k in range(4):
        o_3[k].wait_recv()
        place_out(oc * 8 + ((x - k + 4) % 4) * 2)
    for k in range(1, 4):
        i_2[k - 1].wait_recv()
        ref = iall.at[c * 4 + (z - k + 4) % 4]
        i_3.append(net.put(ref, ref, other))

    @pl.loop(0, n_chunks)
    def _(t):
        k = rows_at(t * CHUNK, CHUNK, CHUNK)
        cg = nt(rhs_o[0:half, :], cot[k, :])
        f = cf[:, k]
        cf[:, k] = f * (cg - jnp.sum(f * cg, axis=0, keepdims=True))

    place_in(c)
    for cp in i_3:
        cp.wait_recv()
    place_in(oc)
    rhs_o[half:, :] = emb[...]

    @pl.loop(0, n_chunks)
    def _(t):
        k = rows_at(t * CHUNK, CHUNK, CHUNK)
        dg = nt(rhs_o[0:half, :], tok[k, :])
        df = jnp.exp(lt[:, k] - l_all[:, 0:1])
        lhs_o[0:half, k] = df.astype(BF16)
        lhs_o[half:, k] = (df * (dg - inner_all[:, 0:1]) + cf[:, k]).astype(BF16)

    H = D // 2
    pieces = ((0, 384), (384, 256))
    c_core = net.group(c_cr)
    for a, b in pieces:
        c_cs[:, a : a + b] = nn(lhs_o[half:, :], tok[:, rows_at(oc * H + a, b, 128)]).astype(BF16)
        c_core.put(c_cs.at[:, a : a + b], c_cr.at[:, a : a + b], other)
    for a, b in pieces:
        c_own[:, a : a + b] = nn(lhs_o[half:, :], tok[:, rows_at(c * H + a, b, 128)])
    c_core.wait_recv()

    @pl.loop(0, 16, unroll=4)
    def _(i):
        r = rows_at(i * 16, 16, 16)
        c_ys[r, :] = (c_own[r, :] + c_cr[r, :].astype(F32)).astype(BF16)

    def block_of(zz, yy):
        return rows_at((yy % 2) * 128 + ((zz % 2) * 2 + yy // 2) * 32 + (zz // 2) * 16, 16, 16)

    c_y = net.group(c_yr.at[pl.ds(1, 15)])
    for a in range(4):
        for b in range(4):
            if a or b:
                zz, yy = (z + a) % 4, (y + b) % 4
                c_y.put(c_ys.at[block_of(zz, yy)], c_yr.at[a * 4 + b], device(zz, yy, x, c))
    c_yr[0] = c_ys[block_of(z, y), :]
    c_y.wait_recv()
    acc = c_yr[0].astype(F32)
    for k in range(1, 16):
        acc = acc + c_yr[k].astype(F32)
    c_xs[0] = acc[0:8]
    c_xs[1] = acc[8:16]
    c_x = net.group(c_xr.at[pl.ds(1, 7)])
    for k in range(4):
        for d in range(2):
            if k or d:
                xx, cc = (x + k) % 4, c if d == 0 else oc
                c_x.put(c_xs.at[xx // 2], c_xr.at[k * 2 + d], device(z, y, xx, cc))
    c_xr[0] = c_xs[x // 2]
    c_x.wait_recv()
    for d in range(2):
        v = c_xr[d] + c_xr[2 + d] + c_xr[4 + d] + c_xr[6 + d]
        k = (x % 2) * 2 + c
        out = v[0:2]
        for i in range(1, 4):
            out = jnp.where(k == i, v[2 * i : 2 * i + 2], out)
        eg_o[:, rows_at((c if d == 0 else oc) * H, H, 128)] = out

    for g in net.groups:
        g.wait_send()


def tn(a, b):
    return lax.dot_general(a, b, (((0,), (0,)), ((), ())), preferred_element_type=F32)


def grads_kernel(eg, lhs, rhs, sin, sgr, hid, pgr, eg_h, tg_h, wi_h, wo_h, tg, wi, wo, sem):
    copies = []

    def store(src, dst):
        cp = pltpu.make_async_copy(src, dst, sem.at[len(copies)])
        cp.start()
        copies.append(cp)

    store(eg, eg_h)
    expert_of = lax.broadcasted_iota(jnp.int32, (16, 1), 0) // 4
    for e in range(wo.shape[0]):
        own = expert_of == e
        wo[e] = tn(jnp.where(own, hid[...].astype(F32), 0.0).astype(BF16), sgr[...]).astype(BF16)
        store(wo.at[e], wo_h.at[e])
        wi[e] = tn(jnp.where(own, sin[...].astype(F32), 0.0).astype(BF16), pgr[...]).astype(BF16)
        store(wi.at[e], wi_h.at[e])
    for t in range(tg.shape[0] // CHUNK):
        k = pl.ds(t * CHUNK, CHUNK)
        tg[k, :] = tn(lhs[:, k], rhs[...]).astype(BF16)
        store(tg.at[k], tg_h.at[k])
    for cp in copies:
        cp.wait()


def on_device(tokens, slot_embed, w_in, w_out, cotangent):
    T, D = tokens.shape
    S = slot_embed.shape[0]
    E, _, F = w_in.shape
    V = pltpu.VMEM
    shape = jax.ShapeDtypeStruct
    blk = (48, 128)
    scratch = [
        V((T, D), BF16), V((S, D), BF16), V(w_in.shape, BF16), V(w_out.shape, BF16), V((T, D), BF16),
        V((S, T), F32), V((S, T), BF16), V((S, T), F32), V((S, T), BF16), V((S, 128), F32), V((S, 128), F32),
        V((128, D), F32), V((128, D + 128), BF16), V((128, D + 128), BF16),
        V((128, D + 128), BF16), V((3, 32, D + 128), BF16), V((8,) + blk, BF16), V((16,) + blk, BF16), V((4,) + blk, BF16),
        V((128, D), F32), V((128, D), BF16), V((128, D), BF16), V((4, 320, 128), BF16), V((3, 320, 128), BF16),
        V((8,) + blk, BF16), V((16,) + blk, BF16), V((4,) + blk, BF16),
        V((4,) + blk, BF16), V((16,) + blk, BF16), V((16, 4) + blk, BF16),
        V((4,) + blk, BF16), V((16,) + blk, BF16), V((8, 8) + blk, BF16),
        V((S, 128), F32), V((S, 128), F32),
        V((S, D // 2), F32), V((S, D // 2), BF16), V((S, D // 2), BF16), V((S, D // 2), BF16),
        V((16, 16, D // 2), BF16), V((2, 8, D // 2), F32), V((8, 8, D // 2), F32),
        pltpu.SemaphoreType.DMA((8,)),
        pltpu.SemaphoreType.DMA((N_GROUPS,)),
        pltpu.SemaphoreType.DMA((N_GROUPS,)),
    ]
    eg, lhs, rhs, slot_in, slot_grad, hidden, pre_grad = pl.pallas_call(
        main_kernel,
        name="moe_exchange",
        out_shape=[
            V((2, D), F32), V((2 * S, T), BF16), V((2 * S, D), BF16),
            V((16, D), BF16), V((16, D), BF16), V((16, F), BF16), V((16, F), BF16),
        ],
        in_specs=[pl.BlockSpec(memory_space=pltpu.HBM)] * 5,
        out_specs=[pl.BlockSpec(memory_space=pltpu.VMEM)] * 7,
        scratch_shapes=scratch,
        compiler_params=pltpu.CompilerParams(
            collective_id=0, has_side_effects=True, vmem_limit_bytes=52 * 2**20
        ),
    )(tokens, slot_embed, w_in, w_out, cotangent)
    embed_grad, token_grad, w_in_grad, w_out_grad = pl.pallas_call(
        grads_kernel,
        name="grads",
        out_shape=[shape((2, D), F32), shape((T, D), BF16), shape(w_in.shape, BF16), shape(w_out.shape, BF16)],
        in_specs=[pl.BlockSpec(memory_space=pltpu.VMEM)] * 7,
        out_specs=[pl.BlockSpec(memory_space=pl.ANY)] * 4,
        scratch_shapes=[
            V((T, D), BF16), V(w_in.shape, BF16), V(w_out.shape, BF16), pltpu.SemaphoreType.DMA((1 + 2 * E + T // CHUNK,)),
        ],
        compiler_params=pltpu.CompilerParams(vmem_limit_bytes=40 * 2**20),
    )(eg, lhs, rhs, slot_in, slot_grad, hidden, pre_grad)
    return (token_grad, embed_grad, w_in_grad, w_out_grad)


def solution(mesh):
    in_specs = (
        P(("seq", "expert"), None),
        P(),
        P("expert", None, "seq"),
        P("expert", "seq", None),
        P(("seq", "expert"), None),
    )
    out_specs = (
        P(("seq", "expert"), None),
        P(("seq", "expert"), None),
        P("expert", None, "seq"),
        P("expert", "seq", None),
    )
    return jax.shard_map(
        on_device, mesh=mesh, in_specs=in_specs, out_specs=out_specs, check_vma=False
    )
```

time: 98.9 us -> 72.9 us (0.74)
  Pallas kernels: 83.2 us -> 72.1 us
  matrix products: 11.1 us -> 0 us
  local copies, waits for them, and re-layouts: 3.62 us -> 0 us
    pallas_call x1 -> x2, Pallas kernels: 83.2 us -> 72.1 us  [the longest x1 67.5 us: on_device(): pl.pallas_call(main_kernel, name='moe_exchange', out_shape=[V((2, D), F32...]
    dot_general x3 -> x0, matrix products: 11.1 us -> none  [the longest x1 4.69 us: on_device(): lax.dot_general(lhs, rhs, (((0,), (0,)), ((), ())), preferred_element_typ...]
    reshape x4 -> x0, local copies, waits for them, and re-layouts: 3.02 us -> none  [grouped(): return v.reshape(E, -1, v.shape[1])]
where the time goes in v2:
time: 72.9 us; the launch traced here: 72.7 us
  Pallas kernels  72.1 us (99%)
    pallas_call x1, Pallas kernels, on_device(): pl.pallas_call(main_kernel, name='moe_exchange', out_shape=[V((2, D), F32...  67.5 us
    pallas_call x1, Pallas kernels, on_device(): pl.pallas_call(grads_kernel, name='grads', out_shape=[shape((2, D), F32),...  4.59 us

profile of v2, /device:TPU:1, one launch (start us, length us, event | category | flops | bytes accessed | tf_op | source)
XLA Modules:
  0.0 72.7 jit_solution(1583723557128986020)
XLA Ops:
  0.6 67.5 %moe_exchange.1 = (f32[2,1280]{1,0:T(2,128)S(1)}, bf16[512,1024]{1,0:T(8,128)(2,1)S(1)}, bf16[512,1280]{1,0:T(8,128)(2,1)S(1)}, bf16[16,1280]{1,0:T(8,128)(2,1)S...) custom-call(bf16[1024,1280]{1,0:T(8,128)(2,1)} %tok_h.1, ...), custom_call_target="tpu_custom_call" | custom-call | tf_op jit(solution)/shard_map/moe_exchange/pallas_call | solution.py:573
  68.2 4.6 %grads.1 = (f32[2,1280]{1,0:T(2,128)}, bf16[1024,1280]{1,0:T(8,128)(2,1)}, bf16[4,1280,384]{2,1,0:T(8,128)(2,1)}, bf16[4,384,1280]{2,1,0:T(8,128)(2,1)}) custom-call(f32[2,1280]{1,0:T(2,128)S(1)} %get-tuple-element.15.eg, bf16[512,1024]{1,0:T(8,128)(2,1)S(1)} %get-tuple-element.16.lhs, bf16[512,1280]{1,0:T(8,128)(2,1)S(1)} %get-tuple-element.17.rhs, ...), custom_call_target="tpu_custom_call" | custom-call | tf_op jit(solution)/shard_map/grads/pallas_call | solution.py:587

commit v3 on v2

--- a/solution.py
+++ b/solution.py
@@ -31,6 +31,20 @@
 
 def nt(a, b):
     return lax.dot_general(a, b, (((1,), (1,)), ((), ())), preferred_element_type=F32)
+
+
+def tn(a, b):
+    return lax.dot_general(a, b, (((0,), (0,)), ((), ())), preferred_element_type=F32)
+
+
+def hops(k):
+    return min(k, 4 - k)
+
+
+PLANE = sorted(
+    ((a, b) for a in range(4) for b in range(4) if a or b), key=lambda p: -hops(p[0]) - hops(p[1])
+)
+RING = (2, 1, 3)
 
 
 def rows_at(start, size, unit):
@@ -115,7 +129,7 @@
 
 def main_kernel(
     tok_h, emb_h, win_h, wout_h, cot_h,
-    eg_o, lhs_o, rhs_o, sin_o, sgr_o, hid_o, pgr_o,
+    eg_o, lhs_o, rhs_o, wi_o, wo_o,
     tok, emb, win, wout, cot,
     lt, et, cf, cb, m_s, s_s,
     u_own, u_cs, u_cr, u_xs, u_xr, u_pk, u_yr, sall,
@@ -158,6 +172,7 @@
     partners += [((z + a) % 4, (y + b) % 4, x, c) for a in range(4) for b in range(4) if a or b]
     partners += [(z, (y + b) % 4, (x + a) % 4, c) for a in range(1, 4) for b in range(4)]
     partners += [(z, y, (x + a) % 4, oc) for a in range(1, 4)]
+    partners += [((z + a) % 4, y, (x + b) % 4, c) for a in range(1, 4) for b in range(1, 4)]
     for p in partners:
         pl.semaphore_signal(barrier, inc=1, device_id=device(*p), device_id_type=MESH)
 
@@ -200,10 +215,9 @@
 
     u_core.wait_recv()
 
-    @pl.loop(0, 8, unroll=4)
-    def _(i):
-        r = rows_at(i * 16, 16, 16)
-        rg = rows_at(c * 128 + i * 16, 16, 16)
+    def merge_core(first):
+        r = rows_at(first, 16, 16)
+        rg = rows_at(c * 128 + first, 16, 16)
         v = u_cr[r, :].astype(F32)
         m1, s1 = m_s[rg, 0:1], s_s[rg, 0:1]
         sc = v[:, D : D + 128]
@@ -218,9 +232,12 @@
         s_s[rg, :] = jnp.broadcast_to(s, (16, 128))
 
     u_x = net.group(u_xr)
-    for k in range(1, 4):
+    for k in RING + (0,):
         xx = (x + k) % 4
-        u_x.put(u_xs.at[rows_at(xx * 32, 32, 32)], u_xr.at[k - 1], device(z, y, xx, c))
+        merge_core(xx * 32)
+        merge_core(xx * 32 + 16)
+        if k:
+            u_x.put(u_xs.at[rows_at(xx * 32, 32, 32)], u_xr.at[k - 1], device(z, y, xx, c))
 
     cot_load = loads["cot"]
     cot_load.wait()
@@ -242,7 +259,7 @@
             g_pk[zz, rows_at(i * 80, 80, 16), :] = jnp.concatenate(tiles, axis=0).astype(BF16)
 
     g_z = net.group(g_zr)
-    for k in range(1, 4):
+    for k in RING:
         zz = (z + k) % 4
         g_z.put(g_pk.at[zz], g_zr.at[k - 1], device(zz, y, x, c))
 
@@ -267,11 +284,9 @@
             tile = scalar_tile([m[8 * h : 8 * h + 8], s[8 * h : 8 * h + 8]])
             u_pk[yy * 4 + zz] = jnp.concatenate(chunk_tiles(u, zz) + [tile], axis=0).astype(BF16)
     u_yz = net.group(u_yr.at[pl.ds(1, 15)])
-    for a in range(4):
-        for b in range(4):
-            if a or b:
-                zz, yy = (z + a) % 4, (y + b) % 4
-                u_yz.put(u_pk.at[(yy % 2) * 4 + zz], u_yr.at[a * 4 + b], device(zz, yy, x, c))
+    for a, b in PLANE:
+        zz, yy = (z + a) % 4, (y + b) % 4
+        u_yz.put(u_pk.at[(yy % 2) * 4 + zz], u_yr.at[a * 4 + b], device(zz, yy, x, c))
     u_yr[0] = u_pk[ylo * 4 + z]
 
     g_z.wait_recv()
@@ -287,11 +302,9 @@
         g_pk2[2 * i + 1] = jnp.concatenate([v[40:], pad], axis=0).astype(BF16)
 
     g_xy = net.group(g_yr.at[pl.ds(1, 15)])
-    for a in range(4):
-        for b in range(4):
-            if a or b:
-                xx, yy = (x + a) % 4, (y + b) % 4
-                g_xy.put(g_pk2.at[xx * 2 + yy % 2], g_yr.at[a * 4 + b], device(z, yy, xx, c))
+    for a, b in PLANE:
+        xx, yy = (x + a) % 4, (y + b) % 4
+        g_xy.put(g_pk2.at[xx * 2 + yy % 2], g_yr.at[a * 4 + b], device(z, yy, xx, c))
     g_yr[0] = g_pk2[x * 2 + ylo]
 
     u_yz.wait_recv()
@@ -308,7 +321,7 @@
         tiles.append(sum(v[8 * j : 8 * j + 8] * f for v, f in zip(parts, fs)) / s)
     sall[z] = jnp.concatenate(tiles + [lse_tile], axis=0).astype(BF16)
     u_ag = net.group(sall.at[pl.ds(0, 3)])
-    for k in range(1, 4):
+    for k in RING:
         u_ag.put(sall.at[z], sall.at[z], device((z + k) % 4, y, x, c))
 
     g_xy.wait_recv()
@@ -317,7 +330,7 @@
         acc = acc + g_yr[k].astype(F32)
     gall[z] = acc.astype(BF16)
     g_ag = net.group(gall.at[pl.ds(0, 3)])
-    for k in range(1, 4):
+    for k in RING:
         g_ag.put(gall.at[z], gall.at[z], device((z + k) % 4, y, x, c))
     loads["win"].wait()
     loads["wout"].wait()
@@ -325,15 +338,14 @@
 
     F = win.shape[2]
     expert_of = lax.broadcasted_iota(jnp.int32, (16, 1), 0) // 4
-    slot_in = jnp.concatenate(unpack_rows([sall[k].astype(F32) for k in range(4)]), axis=1).astype(BF16)
-    sin_o[...] = slot_in
+    slot_in_f = jnp.concatenate(unpack_rows([sall[k].astype(F32) for k in range(4)]), axis=1)
+    slot_in = slot_in_f.astype(BF16)
     pre = jnp.zeros((16, F), F32)
     for e in range(4):
         pre = jnp.where(expert_of == e, nn(slot_in, win[e]), pre)
     th = jnp.tanh(GELU_C * (pre + GELU_A * pre * pre * pre))
     hidden_f = 0.5 * pre * (1.0 + th)
     slope = 0.5 * (1.0 + th) + 0.5 * pre * (1.0 - th * th) * GELU_C * (1.0 + 3.0 * GELU_A * pre * pre)
-    hid_o[...] = hidden_f.astype(BF16)
     out_part = jnp.zeros((16, D), F32)
     for e in range(4):
         out_part += nn(jnp.where(expert_of == e, hidden_f, 0.0).astype(BF16), wout[e])
@@ -343,11 +355,9 @@
 
     def seq_sums(pk, sr):
         group = net.group(sr.at[pl.ds(1, 15)])
-        for a in range(4):
-            for b in range(4):
-                if a or b:
-                    zz = (z + a) % 4
-                    group.put(pk.at[zz], sr.at[a * 4 + b], device(zz, (y + b) % 4, x, c))
+        for a, b in PLANE:
+            zz = (z + a) % 4
+            group.put(pk.at[zz], sr.at[a * 4 + b], device(zz, (y + b) % 4, x, c))
         sr[0] = pk[z]
         return group
 
@@ -363,12 +373,10 @@
     g_ag.wait_recv()
 
     slot_grad = jnp.concatenate(unpack_rows([gall[k].astype(F32) for k in range(4)]), axis=1).astype(BF16)
-    sgr_o[...] = slot_grad
     hid_grad = jnp.zeros((16, F), F32)
     for e in range(4):
         hid_grad = jnp.where(expert_of == e, nt(slot_grad, wout[e]), hid_grad)
     pre_grad = (hid_grad * slope).astype(BF16)
-    pgr_o[...] = pre_grad
     in_part = jnp.zeros((16, D), F32)
     for e in range(4):
         in_part = jnp.where(expert_of == e, nt(pre_grad, win[e]), in_part)
@@ -379,16 +387,21 @@
         i_pk[zz] = jnp.concatenate(chunk_tiles(in_part, zz) + [tile], axis=0).astype(BF16)
     i_seq = seq_sums(i_pk, i_sr)
 
+    for e in range(4):
+        own = expert_of == e
+        wo_o[e] = tn(jnp.where(own, hidden_f, 0.0).astype(BF16), slot_grad).astype(BF16)
+        wi_o[e] = tn(jnp.where(own, slot_in_f, 0.0).astype(BF16), pre_grad).astype(BF16)
+
     o_seq.wait_recv()
     pair = c * 8 + x * 2
     for parity in range(2):
         acc = seq_total(o_sr, parity, 40)
         lse_tile = o_sr[parity, 40:48, :].astype(F32)
         oall[pair + (ylo + parity) % 2, z] = jnp.concatenate([acc, lse_tile], axis=0).astype(BF16)
-    o_1 = net.group(oall.at[pl.ds(0, 2), pl.ds(0, 3)])
-    for k in range(1, 4):
-        ref = oall.at[pl.ds(pair, 2), z]
-        o_1.put(ref, ref, device((z + k) % 4, y, x, c))
+    o_all = [net.group(oall.at[pl.ds(0, 2), pl.ds(0, 3)])] + [net.group(oall.at[pl.ds(0, 2)]) for _ in range(3)]
+    ref = oall.at[pl.ds(pair, 2), z]
+    for k, a in PLANE:
+        o_all[k].put(ref, ref, device((z + a) % 4, y, (x + k) % 4, c))
 
     i_seq.wait_recv()
     cz = c * 4 + z
@@ -397,10 +410,10 @@
         inner = scalar_of(acc[40:48], 0)
         block = jnp.concatenate([acc[:40], scalar_tile([inner])], axis=0)
         iall[cz, x * 2 + (ylo + parity) % 2] = block.astype(BF16)
-    i_1 = net.group(iall.at[0, pl.ds(0, 6)])
-    for k in range(1, 4):
-        ref = iall.at[cz, pl.ds(x * 2, 2)]
-        i_1.put(ref, ref, device(z, y, (x + k) % 4, c))
+    i_all = [net.group(iall.at[0, pl.ds(0, 6)])] + [net.group(iall.at[0]) for _ in range(3)]
+    ref = iall.at[cz, pl.ds(x * 2, 2)]
+    for k, a in PLANE:
+        i_all[k].put(ref, ref, device((z + k) % 4, y, (x + a) % 4, c))
 
     half = rhs_o.shape[0] // 2
 
@@ -420,21 +433,9 @@
         def _(k):
             place(core * 8 + k, [iall[core * 4 + zz, k].astype(F32) for zz in range(4)], inner_all)
 
-    o_1.wait_recv()
-    o_2, o_3 = [], []
-    ref = oall.at[pl.ds(pair, 2)]
-    for k in range(1, 4):
-        o_2.append(net.put(ref, ref, device(z, y, (x + k) % 4, c)))
-    o_3.append(net.put(ref, ref, other))
-    place_out(pair)
-    i_1.wait_recv()
-    i_2, i_3 = [], []
-    ref = iall.at[cz]
-    for k in range(1, 4):
-        i_2.append(net.put(ref, ref, device((z + k) % 4, y, x, c)))
-    i_3.append(net.put(ref, ref, other))
-    for k in range(1, 4):
-        o_2[k - 1].wait_recv()
+    o_3, i_3 = [], []
+    for k in range(4):
+        o_all[k].wait_recv()
         first = c * 8 + ((x - k + 4) % 4) * 2
         ref = oall.at[pl.ds(first, 2)]
         o_3.append(net.put(ref, ref, other))
@@ -442,17 +443,20 @@
     for k in range(4):
         o_3[k].wait_recv()
         place_out(oc * 8 + ((x - k + 4) % 4) * 2)
-    for k in range(1, 4):
-        i_2[k - 1].wait_recv()
+    for k in range(4):
+        i_all[k].wait_recv()
         ref = iall.at[c * 4 + (z - k + 4) % 4]
         i_3.append(net.put(ref, ref, other))
 
-    @pl.loop(0, n_chunks)
+    @pl.loop(0, n_chunks, unroll=2)
     def _(t):
         k = rows_at(t * CHUNK, CHUNK, CHUNK)
         cg = nt(rhs_o[0:half, :], cot[k, :])
         f = cf[:, k]
         cf[:, k] = f * (cg - jnp.sum(f * cg, axis=0, keepdims=True))
+        df = jnp.exp(lt[:, k] - l_all[:, 0:1])
+        lt[:, k] = df
+        lhs_o[0:half, k] = df.astype(BF16)
 
     place_in(c)
     for cp in i_3:
@@ -460,13 +464,11 @@
     place_in(oc)
     rhs_o[half:, :] = emb[...]
 
-    @pl.loop(0, n_chunks)
+    @pl.loop(0, n_chunks, unroll=2)
     def _(t):
         k = rows_at(t * CHUNK, CHUNK, CHUNK)
         dg = nt(rhs_o[0:half, :], tok[k, :])
-        df = jnp.exp(lt[:, k] - l_all[:, 0:1])
-        lhs_o[0:half, k] = df.astype(BF16)
-        lhs_o[half:, k] = (df * (dg - inner_all[:, 0:1]) + cf[:, k]).astype(BF16)
+        lhs_o[half:, k] = (lt[:, k] * (dg - inner_all[:, 0:1]) + cf[:, k]).astype(BF16)
 
     H = D // 2
     pieces = ((0, 384), (384, 256))
@@ -487,43 +489,41 @@
         return rows_at((yy % 2) * 128 + ((zz % 2) * 2 + yy // 2) * 32 + (zz // 2) * 16, 16, 16)
 
     c_y = net.group(c_yr.at[pl.ds(1, 15)])
-    for a in range(4):
-        for b in range(4):
-            if a or b:
-                zz, yy = (z + a) % 4, (y + b) % 4
-                c_y.put(c_ys.at[block_of(zz, yy)], c_yr.at[a * 4 + b], device(zz, yy, x, c))
+    for a, b in PLANE:
+        zz, yy = (z + a) % 4, (y + b) % 4
+        c_y.put(c_ys.at[block_of(zz, yy)], c_yr.at[a * 4 + b], device(zz, yy, x, c))
     c_yr[0] = c_ys[block_of(z, y), :]
     c_y.wait_recv()
     acc = c_yr[0].astype(F32)
     for k in range(1, 16):
         acc = acc + c_yr[k].astype(F32)
-    c_xs[0] = acc[0:8]
-    c_xs[1] = acc[8:16]
+    blocks = H // 128
+    at = lax.broadcasted_iota(jnp.int32, (128, 16 * blocks), 0)
+    of = lax.broadcasted_iota(jnp.int32, (128, 16 * blocks), 1)
+    t_of, r_of = of // 16, of % 16
+    pick = at == (r_of // 2) * 16 + 2 * t_of + r_of % 2
+    stacked = jnp.concatenate([acc[:, 128 * t : 128 * t + 128] for t in range(blocks)], axis=0).astype(BF16)
+    packed = nn(jnp.where(pick, 1.0, 0.0).astype(BF16), stacked)
+    for j in range(8):
+        c_xs[j] = packed[16 * j : 16 * j + 16].astype(BF16)
     c_x = net.group(c_xr.at[pl.ds(1, 7)])
-    for k in range(4):
+    for k in RING + (0,):
         for d in range(2):
             if k or d:
                 xx, cc = (x + k) % 4, c if d == 0 else oc
-                c_x.put(c_xs.at[xx // 2], c_xr.at[k * 2 + d], device(z, y, xx, cc))
-    c_xr[0] = c_xs[x // 2]
+                c_x.put(c_xs.at[xx * 2 + cc], c_xr.at[k * 2 + d], device(z, y, xx, cc))
+    c_xr[0] = c_xs[x * 2 + c]
     c_x.wait_recv()
     for d in range(2):
-        v = c_xr[d] + c_xr[2 + d] + c_xr[4 + d] + c_xr[6 + d]
-        k = (x % 2) * 2 + c
-        out = v[0:2]
-        for i in range(1, 4):
-            out = jnp.where(k == i, v[2 * i : 2 * i + 2], out)
+        v = sum(c_xr[2 * k + d].astype(F32) for k in range(4))
+        out = jnp.concatenate([v[2 * t : 2 * t + 2] for t in range(blocks)], axis=1)
         eg_o[:, rows_at((c if d == 0 else oc) * H, H, 128)] = out
 
     for g in net.groups:
         g.wait_send()
 
 
-def tn(a, b):
-    return lax.dot_general(a, b, (((0,), (0,)), ((), ())), preferred_element_type=F32)
-
-
-def grads_kernel(eg, lhs, rhs, sin, sgr, hid, pgr, eg_h, tg_h, wi_h, wo_h, tg, wi, wo, sem):
+def grads_kernel(eg, lhs, rhs, wi, wo, eg_h, tg_h, wi_h, wo_h, tg, sem):
     copies = []
 
     def store(src, dst):
@@ -531,18 +531,16 @@
         cp.start()
         copies.append(cp)
 
+    store(wi, wi_h)
+    store(wo, wo_h)
     store(eg, eg_h)
-    expert_of = lax.broadcasted_iota(jnp.int32, (16, 1), 0) // 4
-    for e in range(wo.shape[0]):
-        own = expert_of == e
-        wo[e] = tn(jnp.where(own, hid[...].astype(F32), 0.0).astype(BF16), sgr[...]).astype(BF16)
-        store(wo.at[e], wo_h.at[e])
-        wi[e] = tn(jnp.where(own, sin[...].astype(F32), 0.0).astype(BF16), pgr[...]).astype(BF16)
-        store(wi.at[e], wi_h.at[e])
-    for t in range(tg.shape[0] // CHUNK):
+    T = tg.shape[0]
+    for t in range(T // CHUNK):
         k = pl.ds(t * CHUNK, CHUNK)
         tg[k, :] = tn(lhs[:, k], rhs[...]).astype(BF16)
-        store(tg.at[k], tg_h.at[k])
+        if t % 2:
+            k = pl.ds((t - 1) * CHUNK, 2 * CHUNK)
+            store(tg.at[k], tg_h.at[k])
     for cp in copies:
         cp.wait()
 
@@ -565,20 +563,20 @@
         V((4,) + blk, BF16), V((16,) + blk, BF16), V((8, 8) + blk, BF16),
         V((S, 128), F32), V((S, 128), F32),
         V((S, D // 2), F32), V((S, D // 2), BF16), V((S, D // 2), BF16), V((S, D // 2), BF16),
-        V((16, 16, D // 2), BF16), V((2, 8, D // 2), F32), V((8, 8, D // 2), F32),
+        V((16, 16, D // 2), BF16), V((8, 16, 128), BF16), V((8, 16, 128), BF16),
         pltpu.SemaphoreType.DMA((8,)),
         pltpu.SemaphoreType.DMA((N_GROUPS,)),
         pltpu.SemaphoreType.DMA((N_GROUPS,)),
     ]
-    eg, lhs, rhs, slot_in, slot_grad, hidden, pre_grad = pl.pallas_call(
+    eg, lhs, rhs, wi, wo = pl.pallas_call(
         main_kernel,
         name="moe_exchange",
         out_shape=[
             V((2, D), F32), V((2 * S, T), BF16), V((2 * S, D), BF16),
-            V((16, D), BF16), V((16, D), BF16), V((16, F), BF16), V((16, F), BF16),
+            V(w_in.shape, BF16), V(w_out.shape, BF16),
         ],
         in_specs=[pl.BlockSpec(memory_space=pltpu.HBM)] * 5,
-        out_specs=[pl.BlockSpec(memory_space=pltpu.VMEM)] * 7,
+        out_specs=[pl.BlockSpec(memory_space=pltpu.VMEM)] * 5,
         scratch_shapes=scratch,
         compiler_params=pltpu.CompilerParams(
             collective_id=0, has_side_effects=True, vmem_limit_bytes=52 * 2**20
@@ -588,13 +586,13 @@
         grads_kernel,
         name="grads",
         out_shape=[shape((2, D), F32), shape((T, D), BF16), shape(w_in.shape, BF16), shape(w_out.shape, BF16)],
-        in_specs=[pl.BlockSpec(memory_space=pltpu.VMEM)] * 7,
+        in_specs=[pl.BlockSpec(memory_space=pltpu.VMEM)] * 5,
         out_specs=[pl.BlockSpec(memory_space=pl.ANY)] * 4,
         scratch_shapes=[
-            V((T, D), BF16), V(w_in.shape, BF16), V(w_out.shape, BF16), pltpu.SemaphoreType.DMA((1 + 2 * E + T // CHUNK,)),
+            V((T, D), BF16), pltpu.SemaphoreType.DMA((3 + T // (2 * CHUNK),)),
         ],
         compiler_params=pltpu.CompilerParams(vmem_limit_bytes=40 * 2**20),
-    )(eg, lhs, rhs, slot_in, slot_grad, hidden, pre_grad)
+    )(eg, lhs, rhs, wi, wo)
     return (token_grad, embed_grad, w_in_grad, w_out_grad)
 
 

time: 72.9 us -> 69.2 us (0.949)
  Pallas kernels: 72.1 us -> 68.4 us
    pallas_call x1, Pallas kernels: 67.5 us -> 64.4 us  [on_device(): pl.pallas_call(main_kernel, name='moe_exchange', out_shape=[V((2, D), F32...]
where the time goes in v3:
time: 69.2 us; the launch traced here: 69.1 us
  Pallas kernels  68.4 us (99%)
    pallas_call x1, Pallas kernels, on_device(): pl.pallas_call(main_kernel, name='moe_exchange', out_shape=[V((2, D), F32...  64.4 us
    pallas_call x1, Pallas kernels, on_device(): pl.pallas_call(grads_kernel, name='grads', out_shape=[shape((2, D), F32),...  4.09 us

profile of v3, /device:TPU:1, one launch (start us, length us, event | category | flops | bytes accessed | tf_op | source)
XLA Modules:
  0.0 69.1 jit_solution(6915520287715084120)
XLA Ops:
  0.6 64.4 %moe_exchange.1 = (f32[2,1280]{1,0:T(2,128)S(1)}, bf16[512,1024]{1,0:T(8,128)(2,1)S(1)}, bf16[512,1280]{1,0:T(8,128)(2,1)S(1)}, bf16[4,1280,384]{2,1,0:T(8,128)(2,1)S(1)}, bf16[4,384,1280]{2,1,0:T(8,128)(2,1)S(1)}) custom-call(bf16[1024,1280]{1,0:T(8,128)(2,1)} %tok_h.1, bf16[256,1280]{1,0:T(8,128)(2,1)} %emb_h.1, bf16[4,1280,384]{2,1,0:T(8,128)(2,1)} %win_h.1, ...), custom_call_target="tpu_custom_call" | custom-call | tf_op jit(solution)/shard_map/moe_exchange/pallas_call | solution.py:571
  65.0 4.1 %grads.1 = (f32[2,1280]{1,0:T(2,128)}, bf16[1024,1280]{1,0:T(8,128)(2,1)}, bf16[4,1280,384]{2,1,0:T(8,128)(2,1)}, bf16[4,384,1280]{2,1,0:T(8,128)(2,1)}) custom-call(f32[2,1280]{1,0:T(2,128)S(1)} %get-tuple-element.13.eg, bf16[512,1024]{1,0:T(8,128)(2,1)S(1)} %get-tuple-element.14.lhs, bf16[512,1280]{1,0:T(8,128)(2,1)S(1)} %get-tuple-element.15.rhs, ...), custom_call_target="tpu_custom_call" | custom-call | tf_op jit(solution)/shard_map/grads/pallas_call | solution.py:585

commit v4 on v3

--- a/solution.py
+++ b/solution.py
@@ -129,8 +129,9 @@
 
 def main_kernel(
     tok_h, emb_h, win_h, wout_h, cot_h,
-    eg_o, lhs_o, rhs_o, wi_o, wo_o,
-    tok, emb, win, wout, cot,
+    eg_o, tg_o, wi_o, wo_o,
+    lhs, rhs, win_t, wout_t, tok_t, cot_t,
+    tok, emb5, win, wout, cot,
     lt, et, cf, cb, m_s, s_s,
     u_own, u_cs, u_cr, u_xs, u_xr, u_pk, u_yr, sall,
     g_own, g_cs, g_cr, g_pk, g_zr, g_pk2, g_yr, gall,
@@ -154,12 +155,9 @@
         loads[name] = cp
 
     for cc in range(2):
-        for xx in range(4):
-            for yy in range(2):
-                g = yy * 8 + xx * 2 + cc
-                p = cc * 128 + xx * 32 + yy * 16
-                pltpu.make_async_copy(emb_h.at[pl.ds(16 * g, 16)], emb.at[pl.ds(p, 16)], ld.at[0]).start()
-    loads["emb"] = pltpu.make_async_copy(emb_h, emb, ld.at[0])
+        for yy in range(2):
+            pltpu.make_async_copy(emb_h.at[yy, :, cc], emb5.at[cc, :, yy], ld.at[0]).start()
+    loads["emb"] = pltpu.make_async_copy(emb_h, emb5, ld.at[0])
     n_chunks = tok.shape[0] // CHUNK
     for t in range(n_chunks):
         load(("tok", t), tok_h.at[pl.ds(t * CHUNK, CHUNK)], tok.at[pl.ds(t * CHUNK, CHUNK)])
@@ -177,9 +175,10 @@
         pl.semaphore_signal(barrier, inc=1, device_id=device(*p), device_id_type=MESH)
 
     loads["emb"].wait()
+    emb = emb5[...].reshape(-1, D)
     for t in range(n_chunks):
         loads[("tok", t)].wait()
-        lt[:, t * CHUNK : (t + 1) * CHUNK] = nt(emb[...], tok[t * CHUNK : (t + 1) * CHUNK, :])
+        lt[:, t * CHUNK : (t + 1) * CHUNK] = nt(emb, tok[t * CHUNK : (t + 1) * CHUNK, :])
 
     @pl.loop(0, 8, unroll=4)
     def _(i):
@@ -262,6 +261,12 @@
     for k in RING:
         zz = (z + k) % 4
         g_z.put(g_pk.at[zz], g_zr.at[k - 1], device(zz, y, x, c))
+
+    loads["win"].wait()
+    loads["wout"].wait()
+    for e in range(4):
+        wout_t[e] = wout[e].T
+        win_t[e] = win[e].T
 
     u_x.wait_recv()
     for yy in range(2):
@@ -307,6 +312,11 @@
         g_xy.put(g_pk2.at[xx * 2 + yy % 2], g_yr.at[a * 4 + b], device(z, yy, xx, c))
     g_yr[0] = g_pk2[x * 2 + ylo]
 
+    for t in range(n_chunks):
+        k = pl.ds(t * CHUNK, CHUNK)
+        tok_t[:, k] = tok[k, :].T
+        cot_t[:, k] = cot[k, :].T
+
     u_yz.wait_recv()
     parts = [u_yr[k].astype(F32) for k in range(16)]
     ms = [scalar_of(v[40:48], 0) for v in parts]
@@ -332,8 +342,6 @@
     g_ag = net.group(gall.at[pl.ds(0, 3)])
     for k in RING:
         g_ag.put(gall.at[z], gall.at[z], device((z + k) % 4, y, x, c))
-    loads["win"].wait()
-    loads["wout"].wait()
     u_ag.wait_recv()
 
     F = win.shape[2]
@@ -353,12 +361,12 @@
         tile = sall[zz, 40:48, :].astype(F32)
         o_pk[zz] = jnp.concatenate(chunk_tiles(out_part, zz) + [tile], axis=0).astype(BF16)
 
-    def seq_sums(pk, sr):
+    def seq_sums(pk, sr, by_z):
         group = net.group(sr.at[pl.ds(1, 15)])
         for a, b in PLANE:
-            zz = (z + a) % 4
-            group.put(pk.at[zz], sr.at[a * 4 + b], device(zz, (y + b) % 4, x, c))
-        sr[0] = pk[z]
+            zz, yy = (z + a) % 4, (y + b) % 4
+            group.put(pk.at[zz if by_z else yy], sr.at[a * 4 + b], device(zz, yy, x, c))
+        sr[0] = pk[z if by_z else y]
         return group
 
     def seq_total(sr, parity, rows):
@@ -368,24 +376,24 @@
             acc = acc + sr[k, 0:rows, :].astype(F32)
         return acc
 
-    o_seq = seq_sums(o_pk, o_sr)
+    o_seq = seq_sums(o_pk, o_sr, True)
 
     g_ag.wait_recv()
 
     slot_grad = jnp.concatenate(unpack_rows([gall[k].astype(F32) for k in range(4)]), axis=1).astype(BF16)
     hid_grad = jnp.zeros((16, F), F32)
     for e in range(4):
-        hid_grad = jnp.where(expert_of == e, nt(slot_grad, wout[e]), hid_grad)
+        hid_grad = jnp.where(expert_of == e, nn(slot_grad, wout_t[e]), hid_grad)
     pre_grad = (hid_grad * slope).astype(BF16)
     in_part = jnp.zeros((16, D), F32)
     for e in range(4):
-        in_part = jnp.where(expert_of == e, nt(pre_grad, win[e]), in_part)
+        in_part = jnp.where(expert_of == e, nn(pre_grad, win_t[e]), in_part)
     inner_part = jnp.sum(pre * pre_grad.astype(F32), axis=1, keepdims=True)
     for zz in range(4):
         h = zz // 2
         tile = scalar_tile([inner_part[8 * h : 8 * h + 8]])
         i_pk[zz] = jnp.concatenate(chunk_tiles(in_part, zz) + [tile], axis=0).astype(BF16)
-    i_seq = seq_sums(i_pk, i_sr)
+    i_seq = seq_sums(i_pk, i_sr, False)
 
     for e in range(4):
         own = expert_of == e
@@ -404,23 +412,23 @@
         o_all[k].put(ref, ref, device((z + a) % 4, y, (x + k) % 4, c))
 
     i_seq.wait_recv()
-    cz = c * 4 + z
+    cy = c * 4 + y
     for parity in range(2):
         acc = seq_total(i_sr, parity, 48)
         inner = scalar_of(acc[40:48], 0)
         block = jnp.concatenate([acc[:40], scalar_tile([inner])], axis=0)
-        iall[cz, x * 2 + (ylo + parity) % 2] = block.astype(BF16)
+        iall[cy, x * 2 + (ylo + parity) % 2] = block.astype(BF16)
     i_all = [net.group(iall.at[0, pl.ds(0, 6)])] + [net.group(iall.at[0]) for _ in range(3)]
-    ref = iall.at[cz, pl.ds(x * 2, 2)]
+    ref = iall.at[cy, pl.ds(x * 2, 2)]
     for k, a in PLANE:
-        i_all[k].put(ref, ref, device((z + k) % 4, y, (x + a) % 4, c))
-
-    half = rhs_o.shape[0] // 2
+        i_all[k].put(ref, ref, device(z, (y + k) % 4, (x + a) % 4, c))
+
+    half = rhs.shape[0] // 2
 
     def place(i, blocks, scalars):
         r = rows_at(i * 16, 16, 16)
         for j, t in enumerate(unpack_rows(blocks)):
-            rhs_o[r, j * 128 : (j + 1) * 128] = t.astype(BF16)
+            rhs[r, j * 128 : (j + 1) * 128] = t.astype(BF16)
         v = jnp.concatenate([scalar_of(blocks[0][40:48], 0), scalar_of(blocks[2][40:48], 0)], axis=0)
         scalars[r, :] = jnp.broadcast_to(v, (16, 128))
 
@@ -445,39 +453,42 @@
         place_out(oc * 8 + ((x - k + 4) % 4) * 2)
     for k in range(4):
         i_all[k].wait_recv()
-        ref = iall.at[c * 4 + (z - k + 4) % 4]
+        ref = iall.at[c * 4 + (y - k + 4) % 4]
         i_3.append(net.put(ref, ref, other))
 
     @pl.loop(0, n_chunks, unroll=2)
     def _(t):
         k = rows_at(t * CHUNK, CHUNK, CHUNK)
-        cg = nt(rhs_o[0:half, :], cot[k, :])
+        cg = nn(rhs[0:half, :], cot_t[:, k])
         f = cf[:, k]
         cf[:, k] = f * (cg - jnp.sum(f * cg, axis=0, keepdims=True))
         df = jnp.exp(lt[:, k] - l_all[:, 0:1])
         lt[:, k] = df
-        lhs_o[0:half, k] = df.astype(BF16)
-
-    place_in(c)
-    for cp in i_3:
-        cp.wait_recv()
-    place_in(oc)
-    rhs_o[half:, :] = emb[...]
-
-    @pl.loop(0, n_chunks, unroll=2)
-    def _(t):
-        k = rows_at(t * CHUNK, CHUNK, CHUNK)
-        dg = nt(rhs_o[0:half, :], tok[k, :])
-        lhs_o[half:, k] = (lt[:, k] * (dg - inner_all[:, 0:1]) + cf[:, k]).astype(BF16)
+        lhs[0:half, k] = df.astype(BF16)
 
     H = D // 2
     pieces = ((0, 384), (384, 256))
     c_core = net.group(c_cr)
-    for a, b in pieces:
-        c_cs[:, a : a + b] = nn(lhs_o[half:, :], tok[:, rows_at(oc * H + a, b, 128)]).astype(BF16)
-        c_core.put(c_cs.at[:, a : a + b], c_cr.at[:, a : a + b], other)
-    for a, b in pieces:
-        c_own[:, a : a + b] = nn(lhs_o[half:, :], tok[:, rows_at(c * H + a, b, 128)])
+
+    def tail(core):
+        place_in(core)
+        rows = rows_at(core * 128, 128, 128)
+        rows_g = rows_at(half + core * 128, 128, 128)
+        for t in range(n_chunks):
+            k = pl.ds(t * CHUNK, CHUNK)
+            dg = nn(rhs[rows, :], tok_t[:, k])
+            lhs[rows_g, k] = (lt[rows, k] * (dg - inner_all[rows, 0:1]) + cf[rows, k]).astype(BF16)
+        w = lhs[rows_g, :]
+        for a, b in pieces:
+            c_cs[rows, a : a + b] = nn(w, tok[:, rows_at(oc * H + a, b, 128)]).astype(BF16)
+        c_core.put(c_cs.at[rows], c_cr.at[rows], other)
+        for a, b in pieces:
+            c_own[rows, a : a + b] = nn(w, tok[:, rows_at(c * H + a, b, 128)])
+
+    tail(c)
+    for cp in i_3:
+        cp.wait_recv()
+    tail(oc)
     c_core.wait_recv()
 
     @pl.loop(0, 16, unroll=4)
@@ -493,6 +504,10 @@
         zz, yy = (z + a) % 4, (y + b) % 4
         c_y.put(c_ys.at[block_of(zz, yy)], c_yr.at[a * 4 + b], device(zz, yy, x, c))
     c_yr[0] = c_ys[block_of(z, y), :]
+    rhs[half:, :] = emb5[...].reshape(-1, D)
+    for t in range(n_chunks):
+        k = pl.ds(t * CHUNK, CHUNK)
+        tg_o[k, :] = tn(lhs[:, k], rhs[...]).astype(BF16)
     c_y.wait_recv()
     acc = c_yr[0].astype(F32)
     for k in range(1, 16):
@@ -523,24 +538,13 @@
         g.wait_send()
 
 
-def grads_kernel(eg, lhs, rhs, wi, wo, eg_h, tg_h, wi_h, wo_h, tg, sem):
-    copies = []
-
-    def store(src, dst):
-        cp = pltpu.make_async_copy(src, dst, sem.at[len(copies)])
+def write_kernel(eg, tg, wi, wo, eg_h, tg_h, wi_h, wo_h, sem):
+    copies = [
+        pltpu.make_async_copy(src, dst, sem.at[i])
+        for i, (src, dst) in enumerate(((eg, eg_h), (wi, wi_h), (wo, wo_h), (tg, tg_h)))
+    ]
+    for cp in copies:
         cp.start()
-        copies.append(cp)
-
-    store(wi, wi_h)
-    store(wo, wo_h)
-    store(eg, eg_h)
-    T = tg.shape[0]
-    for t in range(T // CHUNK):
-        k = pl.ds(t * CHUNK, CHUNK)
-        tg[k, :] = tn(lhs[:, k], rhs[...]).astype(BF16)
-        if t % 2:
-            k = pl.ds((t - 1) * CHUNK, 2 * CHUNK)
-            store(tg.at[k], tg_h.at[k])
     for cp in copies:
         cp.wait()
 
@@ -553,7 +557,9 @@
     shape = jax.ShapeDtypeStruct
     blk = (48, 128)
     scratch = [
-        V((T, D), BF16), V((S, D), BF16), V(w_in.shape, BF16), V(w_out.shape, BF16), V((T, D), BF16),
+        V((2 * S, T), BF16), V((2 * S, D), BF16),
+        V((E, F, D), BF16), V((E, D, F), BF16), V((D, T), BF16), V((D, T), BF16),
+        V((T, D), BF16), V((2, 4, 2, 16, D), BF16), V(w_in.shape, BF16), V(w_out.shape, BF16), V((T, D), BF16),
         V((S, T), F32), V((S, T), BF16), V((S, T), F32), V((S, T), BF16), V((S, 128), F32), V((S, 128), F32),
         V((128, D), F32), V((128, D + 128), BF16), V((128, D + 128), BF16),
         V((128, D + 128), BF16), V((3, 32, D + 128), BF16), V((8,) + blk, BF16), V((16,) + blk, BF16), V((4,) + blk, BF16),
@@ -568,31 +574,28 @@
         pltpu.SemaphoreType.DMA((N_GROUPS,)),
         pltpu.SemaphoreType.DMA((N_GROUPS,)),
     ]
-    eg, lhs, rhs, wi, wo = pl.pallas_call(
+    outs = pl.pallas_call(
         main_kernel,
         name="moe_exchange",
         out_shape=[
-            V((2, D), F32), V((2 * S, T), BF16), V((2 * S, D), BF16),
-            V(w_in.shape, BF16), V(w_out.shape, BF16),
+            V((2, D), F32), V((T, D), BF16), V(w_in.shape, BF16), V(w_out.shape, BF16),
         ],
         in_specs=[pl.BlockSpec(memory_space=pltpu.HBM)] * 5,
-        out_specs=[pl.BlockSpec(memory_space=pltpu.VMEM)] * 5,
+        out_specs=[pl.BlockSpec(memory_space=pltpu.VMEM)] * 4,
         scratch_shapes=scratch,
         compiler_params=pltpu.CompilerParams(
             collective_id=0, has_side_effects=True, vmem_limit_bytes=52 * 2**20
         ),
-    )(tokens, slot_embed, w_in, w_out, cotangent)
+    )(tokens, slot_embed.reshape(2, 4, 2, 16, D), w_in, w_out, cotangent)
     embed_grad, token_grad, w_in_grad, w_out_grad = pl.pallas_call(
-        grads_kernel,
-        name="grads",
+        write_kernel,
+        name="write",
         out_shape=[shape((2, D), F32), shape((T, D), BF16), shape(w_in.shape, BF16), shape(w_out.shape, BF16)],
-        in_specs=[pl.BlockSpec(memory_space=pltpu.VMEM)] * 5,
+        in_specs=[pl.BlockSpec(memory_space=pltpu.VMEM)] * 4,
         out_specs=[pl.BlockSpec(memory_space=pl.ANY)] * 4,
-        scratch_shapes=[
-            V((T, D), BF16), pltpu.SemaphoreType.DMA((3 + T // (2 * CHUNK),)),
-        ],
+        scratch_shapes=[pltpu.SemaphoreType.DMA((4,))],
         compiler_params=pltpu.CompilerParams(vmem_limit_bytes=40 * 2**20),
-    )(eg, lhs, rhs, wi, wo)
+    )(*outs)
     return (token_grad, embed_grad, w_in_grad, w_out_grad)
 
 

time: 69.2 us -> 66.7 us (0.964)
  Pallas kernels: 68.4 us -> 65.8 us
    pallas_call x1, Pallas kernels: 64.4 us -> 61.7 us  [on_device(): pl.pallas_call(main_kernel, name='moe_exchange', out_shape=[V((2, D), F32...]
where the time goes in v4:
time: 66.7 us; the launch traced here: 66.6 us
  Pallas kernels  65.8 us (99%)
  between operations  0.8 us (1%)
    pallas_call x1, Pallas kernels, on_device(): pl.pallas_call(main_kernel, name='moe_exchange', out_shape=[V((2, D), F32...  61.7 us
    pallas_call x1, Pallas kernels, on_device(): pl.pallas_call(write_kernel, name='write', out_shape=[shape((2, D), F32),...  4.12 us

profile of v4, /device:TPU:1, one launch (start us, length us, event | category | flops | bytes accessed | tf_op | source)
XLA Modules:
  0.0 66.6 jit_solution(9308303915216360742)
XLA Ops:
  0.6 61.7 %moe_exchange.1 = (f32[2,1280]{1,0:T(2,128)S(1)}, bf16[1024,1280]{1,0:T(8,128)(2,1)S(1)}, bf16[4,1280,384]{2,1,0:T(8,128)(2,1)S(1)}, bf16[4,384,1280]{2,1,0:T(8,128)(2,1)S(1)}) custom-call(bf16[1024,1280]{1,0:T(8,128)(2,1)} %tok_h.1, bf16[2,4,2,16,1280]{4,3,2,1,0:T(8,128)(2,1)} %bitcast.1, bf16[4,1280,384]{2,1,0:T(8,128)(2,1)} %win_h.1, ...), custom_call_target="tpu_custom_call" | custom-call | tf_op jit(solution)/shard_map/moe_exchange/pallas_call | solution.py:577
  62.3 4.1 %write.1 = (f32[2,1280]{1,0:T(2,128)}, bf16[1024,1280]{1,0:T(8,128)(2,1)}, bf16[4,1280,384]{2,1,0:T(8,128)(2,1)}, bf16[4,384,1280]{2,1,0:T(8,128)(2,1)}) custom-call(f32[2,1280]{1,0:T(2,128)S(1)} %get-tuple-element.12.eg, bf16[1024,1280]{1,0:T(8,128)(2,1)S(1)} %get-tuple-element.13.tg, bf16[4,1280,384]{2,1,0:T(8,128)(2,1)S(1)} %get-tuple-element.14.wi, ...), custom_call_target="tpu_custom_call" | custom-call | tf_op jit(solution)/shard_map/write/pallas_call | solution.py:590

commit v5 on v4

--- a/solution.py
+++ b/solution.py
@@ -180,6 +180,26 @@
         loads[("tok", t)].wait()
         lt[:, t * CHUNK : (t + 1) * CHUNK] = nt(emb, tok[t * CHUNK : (t + 1) * CHUNK, :])
 
+    ro = rows_at(oc * 128, 128, 128)
+    rc = rows_at(c * 128, 128, 128)
+
+    @pl.loop(0, n_chunks, unroll=2)
+    def _(t):
+        k = rows_at(t * CHUNK, CHUNK, CHUNK)
+        l = lt[:, k]
+        e = jnp.exp(l - jnp.max(l, axis=0, keepdims=True))
+        f = e / jnp.sum(e, axis=0, keepdims=True)
+        cf[:, k] = f
+        cb[:, k] = f.astype(BF16)
+
+    cot_load = loads["cot"]
+    cot_load.wait()
+    w_o = cb[ro, :]
+    for n in range(D // 256):
+        g_cs[:, n * 256 : (n + 1) * 256] = nn(w_o, cot[:, n * 256 : (n + 1) * 256]).astype(BF16)
+    pl.semaphore_wait(barrier, len(partners))
+    g_core = net.put(g_cs, g_cr, device(z, y, x, oc))
+
     @pl.loop(0, 8, unroll=4)
     def _(i):
         r = rows_at(i * 32, 32, 32)
@@ -191,26 +211,32 @@
         m_s[r, :] = jnp.broadcast_to(m, (32, 128))
         s_s[r, :] = jnp.broadcast_to(s, (32, 128))
 
-    ro = rows_at(oc * 128, 128, 128)
-    rc = rows_at(c * 128, 128, 128)
     w_o = et[ro, :]
     for n in range(D // 256):
         u_cs[:, n * 256 : (n + 1) * 256] = nn(w_o, tok[:, n * 256 : (n + 1) * 256]).astype(BF16)
     u_cs[:, D : D + 128] = scalar_tile([m_s[ro, 0:1], s_s[ro, 0:1]]).astype(BF16)
-    pl.semaphore_wait(barrier, len(partners))
     u_core = net.put(u_cs, u_cr, device(z, y, x, oc))
+    w_c = cb[rc, :]
+    for n in range(D // 256):
+        g_own[:, n * 256 : (n + 1) * 256] = nn(w_c, cot[:, n * 256 : (n + 1) * 256])
+    g_core.wait_recv()
+
+    @pl.loop(0, 4, unroll=2)
+    def _(i):
+        r = rows_at(i * 32, 32, 32)
+        v = g_own[r, :] + g_cr[r, :].astype(F32)
+        for zz in range(4):
+            tiles = chunk_tiles(v[:16], zz) + chunk_tiles(v[16:], zz)
+            g_pk[zz, rows_at(i * 80, 80, 16), :] = jnp.concatenate(tiles, axis=0).astype(BF16)
+
+    g_z = net.group(g_zr)
+    for k in RING:
+        zz = (z + k) % 4
+        g_z.put(g_pk.at[zz], g_zr.at[k - 1], device(zz, y, x, c))
+
     w_c = et[rc, :]
     for n in range(D // 256):
         u_own[:, n * 256 : (n + 1) * 256] = nn(w_c, tok[:, n * 256 : (n + 1) * 256])
-
-    @pl.loop(0, n_chunks)
-    def _(t):
-        k = rows_at(t * CHUNK, CHUNK, CHUNK)
-        l = lt[:, k]
-        e = jnp.exp(l - jnp.max(l, axis=0, keepdims=True))
-        f = e / jnp.sum(e, axis=0, keepdims=True)
-        cf[:, k] = f
-        cb[:, k] = f.astype(BF16)
 
     u_core.wait_recv()
 
@@ -238,35 +264,29 @@
         if k:
             u_x.put(u_xs.at[rows_at(xx * 32, 32, 32)], u_xr.at[k - 1], device(z, y, xx, c))
 
-    cot_load = loads["cot"]
-    cot_load.wait()
-    w_o = cb[ro, :]
-    for n in range(D // 256):
-        g_cs[:, n * 256 : (n + 1) * 256] = nn(w_o, cot[:, n * 256 : (n + 1) * 256]).astype(BF16)
-    g_core = net.put(g_cs, g_cr, device(z, y, x, oc))
-    w_c = cb[rc, :]
-    for n in range(D // 256):
-        g_own[:, n * 256 : (n + 1) * 256] = nn(w_c, cot[:, n * 256 : (n + 1) * 256])
-    g_core.wait_recv()
-
-    @pl.loop(0, 4, unroll=2)
-    def _(i):
-        r = rows_at(i * 32, 32, 32)
-        v = g_own[r, :] + g_cr[r, :].astype(F32)
-        for zz in range(4):
-            tiles = chunk_tiles(v[:16], zz) + chunk_tiles(v[16:], zz)
-            g_pk[zz, rows_at(i * 80, 80, 16), :] = jnp.concatenate(tiles, axis=0).astype(BF16)
-
-    g_z = net.group(g_zr)
-    for k in RING:
-        zz = (z + k) % 4
-        g_z.put(g_pk.at[zz], g_zr.at[k - 1], device(zz, y, x, c))
-
     loads["win"].wait()
     loads["wout"].wait()
     for e in range(4):
         wout_t[e] = wout[e].T
         win_t[e] = win[e].T
+
+    g_z.wait_recv()
+
+    @pl.loop(0, 4, unroll=2)
+    def _(i):
+        r = rows_at(i * 80, 80, 16)
+        v = g_pk[z, r, :].astype(F32)
+        for k in range(3):
+            v = v + g_zr[k, r, :].astype(F32)
+        pad = jnp.zeros(TILE0, F32)
+        g_pk2[2 * i] = jnp.concatenate([v[:40], pad], axis=0).astype(BF16)
+        g_pk2[2 * i + 1] = jnp.concatenate([v[40:], pad], axis=0).astype(BF16)
+
+    g_xy = net.group(g_yr.at[pl.ds(1, 15)])
+    for a, b in PLANE:
+        xx, yy = (x + a) % 4, (y + b) % 4
+        g_xy.put(g_pk2.at[xx * 2 + yy % 2], g_yr.at[a * 4 + b], device(z, yy, xx, c))
+    g_yr[0] = g_pk2[x * 2 + ylo]
 
     u_x.wait_recv()
     for yy in range(2):
@@ -284,38 +304,30 @@
         fs = [jnp.exp(mk - m) for mk in ms]
         s = sum(a * f for a, f in zip(sums, fs))
         u = sum(a * f for a, f in zip(us, fs))
+        tile = scalar_tile([m, s])
         for zz in range(4):
             h = zz // 2
-            tile = scalar_tile([m[8 * h : 8 * h + 8], s[8 * h : 8 * h + 8]])
-            u_pk[yy * 4 + zz] = jnp.concatenate(chunk_tiles(u, zz) + [tile], axis=0).astype(BF16)
+            tiles = chunk_tiles(u, zz) + [tile[8 * h : 8 * h + 8]]
+            u_pk[yy * 4 + zz] = jnp.concatenate(tiles, axis=0).astype(BF16)
     u_yz = net.group(u_yr.at[pl.ds(1, 15)])
     for a, b in PLANE:
         zz, yy = (z + a) % 4, (y + b) % 4
         u_yz.put(u_pk.at[(yy % 2) * 4 + zz], u_yr.at[a * 4 + b], device(zz, yy, x, c))
     u_yr[0] = u_pk[ylo * 4 + z]
 
-    g_z.wait_recv()
-
-    @pl.loop(0, 4, unroll=2)
-    def _(i):
-        r = rows_at(i * 80, 80, 16)
-        v = g_pk[z, r, :].astype(F32)
-        for k in range(3):
-            v = v + g_zr[k, r, :].astype(F32)
-        pad = jnp.zeros(TILE0, F32)
-        g_pk2[2 * i] = jnp.concatenate([v[:40], pad], axis=0).astype(BF16)
-        g_pk2[2 * i + 1] = jnp.concatenate([v[40:], pad], axis=0).astype(BF16)
-
-    g_xy = net.group(g_yr.at[pl.ds(1, 15)])
-    for a, b in PLANE:
-        xx, yy = (x + a) % 4, (y + b) % 4
-        g_xy.put(g_pk2.at[xx * 2 + yy % 2], g_yr.at[a * 4 + b], device(z, yy, xx, c))
-    g_yr[0] = g_pk2[x * 2 + ylo]
-
     for t in range(n_chunks):
         k = pl.ds(t * CHUNK, CHUNK)
         tok_t[:, k] = tok[k, :].T
         cot_t[:, k] = cot[k, :].T
+
+    g_xy.wait_recv()
+    acc = g_yr[0].astype(F32)
+    for k in range(1, 16):
+        acc = acc + g_yr[k].astype(F32)
+    gall[z] = acc.astype(BF16)
+    g_ag = net.group(gall.at[pl.ds(0, 3)])
+    for k in RING:
+        g_ag.put(gall.at[z], gall.at[z], device((z + k) % 4, y, x, c))
 
     u_yz.wait_recv()
     parts = [u_yr[k].astype(F32) for k in range(16)]
@@ -334,33 +346,6 @@
     for k in RING:
         u_ag.put(sall.at[z], sall.at[z], device((z + k) % 4, y, x, c))
 
-    g_xy.wait_recv()
-    acc = g_yr[0].astype(F32)
-    for k in range(1, 16):
-        acc = acc + g_yr[k].astype(F32)
-    gall[z] = acc.astype(BF16)
-    g_ag = net.group(gall.at[pl.ds(0, 3)])
-    for k in RING:
-        g_ag.put(gall.at[z], gall.at[z], device((z + k) % 4, y, x, c))
-    u_ag.wait_recv()
-
-    F = win.shape[2]
-    expert_of = lax.broadcasted_iota(jnp.int32, (16, 1), 0) // 4
-    slot_in_f = jnp.concatenate(unpack_rows([sall[k].astype(F32) for k in range(4)]), axis=1)
-    slot_in = slot_in_f.astype(BF16)
-    pre = jnp.zeros((16, F), F32)
-    for e in range(4):
-        pre = jnp.where(expert_of == e, nn(slot_in, win[e]), pre)
-    th = jnp.tanh(GELU_C * (pre + GELU_A * pre * pre * pre))
-    hidden_f = 0.5 * pre * (1.0 + th)
-    slope = 0.5 * (1.0 + th) + 0.5 * pre * (1.0 - th * th) * GELU_C * (1.0 + 3.0 * GELU_A * pre * pre)
-    out_part = jnp.zeros((16, D), F32)
-    for e in range(4):
-        out_part += nn(jnp.where(expert_of == e, hidden_f, 0.0).astype(BF16), wout[e])
-    for zz in range(4):
-        tile = sall[zz, 40:48, :].astype(F32)
-        o_pk[zz] = jnp.concatenate(chunk_tiles(out_part, zz) + [tile], axis=0).astype(BF16)
-
     def seq_sums(pk, sr, by_z):
         group = net.group(sr.at[pl.ds(1, 15)])
         for a, b in PLANE:
@@ -376,23 +361,44 @@
             acc = acc + sr[k, 0:rows, :].astype(F32)
         return acc
 
-    o_seq = seq_sums(o_pk, o_sr, True)
-
+    F = win.shape[2]
+    expert_of = lax.broadcasted_iota(jnp.int32, (16, 1), 0) // 4
     g_ag.wait_recv()
-
     slot_grad = jnp.concatenate(unpack_rows([gall[k].astype(F32) for k in range(4)]), axis=1).astype(BF16)
     hid_grad = jnp.zeros((16, F), F32)
     for e in range(4):
         hid_grad = jnp.where(expert_of == e, nn(slot_grad, wout_t[e]), hid_grad)
-    pre_grad = (hid_grad * slope).astype(BF16)
+    u_ag.wait_recv()
+    slot_in_f = jnp.concatenate(unpack_rows([sall[k].astype(F32) for k in range(4)]), axis=1)
+    slot_in = slot_in_f.astype(BF16)
+    pre = jnp.zeros((16, F), F32)
+    hidden_f = jnp.zeros((16, F), F32)
+    pre_grad = jnp.zeros((16, F), F32)
+    out_part = jnp.zeros((16, D), F32)
+    for e in range(4):
+        own = expert_of == e
+        v = nn(slot_in, win[e])
+        th = jnp.tanh(GELU_C * (v + GELU_A * v * v * v))
+        act = jnp.where(own, 0.5 * v * (1.0 + th), 0.0)
+        slope = 0.5 * (1.0 + th) + 0.5 * v * (1.0 - th * th) * GELU_C * (1.0 + 3.0 * GELU_A * v * v)
+        out_part += nn(act.astype(BF16), wout[e])
+        hidden_f += act
+        pre = jnp.where(own, v, pre)
+        pre_grad += jnp.where(own, hid_grad * slope, 0.0)
+    for zz in range(4):
+        tile = sall[zz, 40:48, :].astype(F32)
+        o_pk[zz] = jnp.concatenate(chunk_tiles(out_part, zz) + [tile], axis=0).astype(BF16)
+    o_seq = seq_sums(o_pk, o_sr, True)
     in_part = jnp.zeros((16, D), F32)
     for e in range(4):
-        in_part = jnp.where(expert_of == e, nn(pre_grad, win_t[e]), in_part)
+        in_part += nn(jnp.where(expert_of == e, pre_grad, 0.0).astype(BF16), win_t[e])
+    pre_grad = pre_grad.astype(BF16)
     inner_part = jnp.sum(pre * pre_grad.astype(F32), axis=1, keepdims=True)
+    tile = scalar_tile([inner_part])
     for zz in range(4):
         h = zz // 2
-        tile = scalar_tile([inner_part[8 * h : 8 * h + 8]])
-        i_pk[zz] = jnp.concatenate(chunk_tiles(in_part, zz) + [tile], axis=0).astype(BF16)
+        tiles = chunk_tiles(in_part, zz) + [tile[8 * h : 8 * h + 8]]
+        i_pk[zz] = jnp.concatenate(tiles, axis=0).astype(BF16)
     i_seq = seq_sums(i_pk, i_sr, False)
 
     for e in range(4):
@@ -437,7 +443,7 @@
             place(first + i, [oall[first + i, k].astype(F32) for k in range(4)], l_all)
 
     def place_in(core):
-        @pl.loop(0, 8, unroll=4)
+        @pl.loop(0, 8, unroll=8)
         def _(k):
             place(core * 8 + k, [iall[core * 4 + zz, k].astype(F32) for zz in range(4)], inner_all)
 
@@ -594,7 +600,7 @@
         in_specs=[pl.BlockSpec(memory_space=pltpu.VMEM)] * 4,
         out_specs=[pl.BlockSpec(memory_space=pl.ANY)] * 4,
         scratch_shapes=[pltpu.SemaphoreType.DMA((4,))],
-        compiler_params=pltpu.CompilerParams(vmem_limit_bytes=40 * 2**20),
+        compiler_params=pltpu.CompilerParams(has_side_effects=True, vmem_limit_bytes=8 * 2**20),
     )(*outs)
     return (token_grad, embed_grad, w_in_grad, w_out_grad)
 

time: 66.7 us -> 65.2 us (0.978)
  Pallas kernels: 65.8 us -> 64.3 us
    pallas_call x1, Pallas kernels: 61.7 us -> 60.2 us  [on_device(): pl.pallas_call(main_kernel, name='moe_exchange', out_shape=[V((2, D), F32...]
where the time goes in v5:
time: 65.2 us; the launch traced here: 65.1 us
  Pallas kernels  64.3 us (99%)
  between operations  0.8 us (1%)
    pallas_call x1, Pallas kernels, on_device(): pl.pallas_call(main_kernel, name='moe_exchange', out_shape=[V((2, D), F32...  60.2 us
    pallas_call x1, Pallas kernels, on_device(): pl.pallas_call(write_kernel, name='write', out_shape=[shape((2, D), F32),...  4.12 us

profile of v5, /device:TPU:1, one launch (start us, length us, event | category | flops | bytes accessed | tf_op | source)
XLA Modules:
  0.0 65.1 jit_solution(10380572130305052340)
XLA Ops:
  0.6 60.2 %moe_exchange.1 = (f32[2,1280]{1,0:T(2,128)S(1)}, bf16[1024,1280]{1,0:T(8,128)(2,1)S(1)}, bf16[4,1280,384]{2,1,0:T(8,128)(2,1)S(1)}, bf16[4,384,1280]{2,1,0:T(8,128)(2,1)S(1)}) custom-call(bf16[1024,1280]{1,0:T(8,128)(2,1)} %tok_h.1, bf16[2,4,2,16,1280]{4,3,2,1,0:T(8,128)(2,1)} %bitcast.1, bf16[4,1280,384]{2,1,0:T(8,128)(2,1)} %win_h.1, ...), custom_call_target="tpu_custom_call" | custom-call | tf_op jit(solution)/shard_map/moe_exchange/pallas_call | solution.py:583
  60.9 4.1 %write.1 = (f32[2,1280]{1,0:T(2,128)}, bf16[1024,1280]{1,0:T(8,128)(2,1)}, bf16[4,1280,384]{2,1,0:T(8,128)(2,1)}, bf16[4,384,1280]{2,1,0:T(8,128)(2,1)}) custom-call(f32[2,1280]{1,0:T(2,128)S(1)} %get-tuple-element.12.eg, bf16[1024,1280]{1,0:T(8,128)(2,1)S(1)} %get-tuple-element.13.tg, bf16[4,1280,384]{2,1,0:T(8,128)(2,1)S(1)} %get-tuple-element.14.wi, ...), custom_call_target="tpu_custom_call" | custom-call | tf_op jit(solution)/shard_map/write/pallas_call | solution.py:596

commit v6 on v5

--- a/solution.py
+++ b/solution.py
@@ -130,7 +130,7 @@
 def main_kernel(
     tok_h, emb_h, win_h, wout_h, cot_h,
     eg_o, tg_o, wi_o, wo_o,
-    lhs, rhs, win_t, wout_t, tok_t, cot_t,
+    lhs, rhs, win_t, wout_t, tok_t, cot_t, p_s, r_s,
     tok, emb5, win, wout, cot,
     lt, et, cf, cb, m_s, s_s,
     u_own, u_cs, u_cr, u_xs, u_xr, u_pk, u_yr, sall,
@@ -183,7 +183,7 @@
     ro = rows_at(oc * 128, 128, 128)
     rc = rows_at(c * 128, 128, 128)
 
-    @pl.loop(0, n_chunks, unroll=2)
+    @pl.loop(0, n_chunks, unroll=4)
     def _(t):
         k = rows_at(t * CHUNK, CHUNK, CHUNK)
         l = lt[:, k]
@@ -200,7 +200,7 @@
     pl.semaphore_wait(barrier, len(partners))
     g_core = net.put(g_cs, g_cr, device(z, y, x, oc))
 
-    @pl.loop(0, 8, unroll=4)
+    @pl.loop(0, 8, unroll=8)
     def _(i):
         r = rows_at(i * 32, 32, 32)
         l = lt[r, :]
@@ -356,9 +356,9 @@
 
     def seq_total(sr, parity, rows):
         ks = [a * 4 + b for a in range(4) for b in range(4) if b % 2 == parity]
-        acc = sr[ks[0], 0:rows, :].astype(F32)
+        acc = sr[ks[0]].astype(F32)[:rows]
         for k in ks[1:]:
-            acc = acc + sr[k, 0:rows, :].astype(F32)
+            acc = acc + sr[k].astype(F32)[:rows]
         return acc
 
     F = win.shape[2]
@@ -386,7 +386,7 @@
         pre = jnp.where(own, v, pre)
         pre_grad += jnp.where(own, hid_grad * slope, 0.0)
     for zz in range(4):
-        tile = sall[zz, 40:48, :].astype(F32)
+        tile = sall[zz].astype(F32)[40:48]
         o_pk[zz] = jnp.concatenate(chunk_tiles(out_part, zz) + [tile], axis=0).astype(BF16)
     o_seq = seq_sums(o_pk, o_sr, True)
     in_part = jnp.zeros((16, D), F32)
@@ -410,7 +410,7 @@
     pair = c * 8 + x * 2
     for parity in range(2):
         acc = seq_total(o_sr, parity, 40)
-        lse_tile = o_sr[parity, 40:48, :].astype(F32)
+        lse_tile = o_sr[parity].astype(F32)[40:48]
         oall[pair + (ylo + parity) % 2, z] = jnp.concatenate([acc, lse_tile], axis=0).astype(BF16)
     o_all = [net.group(oall.at[pl.ds(0, 2), pl.ds(0, 3)])] + [net.group(oall.at[pl.ds(0, 2)]) for _ in range(3)]
     ref = oall.at[pl.ds(pair, 2), z]
@@ -450,27 +450,33 @@
     o_3, i_3 = [], []
     for k in range(4):
         o_all[k].wait_recv()
-        first = c * 8 + ((x - k + 4) % 4) * 2
-        ref = oall.at[pl.ds(first, 2)]
+        ref = oall.at[pl.ds(c * 8 + ((x - k + 4) % 4) * 2, 2)]
         o_3.append(net.put(ref, ref, other))
-        place_out(first)
     for k in range(4):
-        o_3[k].wait_recv()
-        place_out(oc * 8 + ((x - k + 4) % 4) * 2)
+        place_out(c * 8 + k * 2)
+
+    def comb(core, first):
+        rows = rows_at(core * 128, 128, 128)
+        for t in range(n_chunks):
+            k = pl.ds(t * CHUNK, CHUNK)
+            p = cf[rows, k] * nn(rhs[rows, :], cot_t[:, k])
+            total = jnp.sum(p, axis=0, keepdims=True)
+            p_s[rows, k] = p
+            r_s[:, k] = total if first else r_s[:, k] + total
+            df = jnp.exp(lt[rows, k] - l_all[rows, 0:1])
+            lt[rows, k] = df
+            lhs[rows, k] = df.astype(BF16)
+
+    comb(c, True)
     for k in range(4):
         i_all[k].wait_recv()
         ref = iall.at[c * 4 + (y - k + 4) % 4]
         i_3.append(net.put(ref, ref, other))
-
-    @pl.loop(0, n_chunks, unroll=2)
-    def _(t):
-        k = rows_at(t * CHUNK, CHUNK, CHUNK)
-        cg = nn(rhs[0:half, :], cot_t[:, k])
-        f = cf[:, k]
-        cf[:, k] = f * (cg - jnp.sum(f * cg, axis=0, keepdims=True))
-        df = jnp.exp(lt[:, k] - l_all[:, 0:1])
-        lt[:, k] = df
-        lhs[0:half, k] = df.astype(BF16)
+    for k in range(4):
+        o_3[k].wait_recv()
+    for k in range(4):
+        place_out(oc * 8 + k * 2)
+    comb(oc, False)
 
     H = D // 2
     pieces = ((0, 384), (384, 256))
@@ -483,7 +489,8 @@
         for t in range(n_chunks):
             k = pl.ds(t * CHUNK, CHUNK)
             dg = nn(rhs[rows, :], tok_t[:, k])
-            lhs[rows_g, k] = (lt[rows, k] * (dg - inner_all[rows, 0:1]) + cf[rows, k]).astype(BF16)
+            lc = p_s[rows, k] - cf[rows, k] * r_s[:, k]
+            lhs[rows_g, k] = (lt[rows, k] * (dg - inner_all[rows, 0:1]) + lc).astype(BF16)
         w = lhs[rows_g, :]
         for a, b in pieces:
             c_cs[rows, a : a + b] = nn(w, tok[:, rows_at(oc * H + a, b, 128)]).astype(BF16)
@@ -564,7 +571,7 @@
     blk = (48, 128)
     scratch = [
         V((2 * S, T), BF16), V((2 * S, D), BF16),
-        V((E, F, D), BF16), V((E, D, F), BF16), V((D, T), BF16), V((D, T), BF16),
+        V((E, F, D), BF16), V((E, D, F), BF16), V((D, T), BF16), V((D, T), BF16), V((S, T), F32), V((1, T), F32),
         V((T, D), BF16), V((2, 4, 2, 16, D), BF16), V(w_in.shape, BF16), V(w_out.shape, BF16), V((T, D), BF16),
         V((S, T), F32), V((S, T), BF16), V((S, T), F32), V((S, T), BF16), V((S, 128), F32), V((S, 128), F32),
         V((128, D), F32), V((128, D + 128), BF16), V((128, D + 128), BF16),

time: 65.2 us -> 64.8 us (level)
  no operation moved by 1% of the time
where the time goes in v6:
time: 64.8 us; the launch traced here: 64.7 us
  Pallas kernels  63.9 us (99%)
  between operations  0.8 us (1%)
    pallas_call x1, Pallas kernels, on_device(): pl.pallas_call(main_kernel, name='moe_exchange', out_shape=[V((2, D), F32...  59.7 us
    pallas_call x1, Pallas kernels, on_device(): pl.pallas_call(write_kernel, name='write', out_shape=[shape((2, D), F32),...  4.12 us

profile of v6, /device:TPU:1, one launch (start us, length us, event | category | flops | bytes accessed | tf_op | source)
XLA Modules:
  0.0 64.7 jit_solution(4904431045019315611)
XLA Ops:
  0.6 59.7 %moe_exchange.1 = (f32[2,1280]{1,0:T(2,128)S(1)}, bf16[1024,1280]{1,0:T(8,128)(2,1)S(1)}, bf16[4,1280,384]{2,1,0:T(8,128)(2,1)S(1)}, bf16[4,384,1280]{2,1,0:T(8,128)(2,1)S(1)}) custom-call(bf16[1024,1280]{1,0:T(8,128)(2,1)} %tok_h.1, bf16[2,4,2,16,1280]{4,3,2,1,0:T(8,128)(2,1)} %bitcast.1, bf16[4,1280,384]{2,1,0:T(8,128)(2,1)} %win_h.1, ...), custom_call_target="tpu_custom_call" | custom-call | tf_op jit(solution)/shard_map/moe_exchange/pallas_call | solution.py:590
  60.4 4.1 %write.1 = (f32[2,1280]{1,0:T(2,128)}, bf16[1024,1280]{1,0:T(8,128)(2,1)}, bf16[4,1280,384]{2,1,0:T(8,128)(2,1)}, bf16[4,384,1280]{2,1,0:T(8,128)(2,1)}) custom-call(f32[2,1280]{1,0:T(2,128)S(1)} %get-tuple-element.12.eg, bf16[1024,1280]{1,0:T(8,128)(2,1)S(1)} %get-tuple-element.13.tg, bf16[4,1280,384]{2,1,0:T(8,128)(2,1)S(1)} %get-tuple-element.14.wi, ...), custom_call_target="tpu_custom_call" | custom-call | tf_op jit(solution)/shard_map/write/pallas_call | solution.py:603
